TPU v7x, 32 devices: a whole 2x2x4 slice. The times are simulated.
32 devices in a mesh: wide: 16 (over z, x, core), kv: 2 (over y).
Axes of the slice: x: 2, y: 2, z: 4, core: 2. Of those that a mesh axis runs over, the one named last changes fastest.
Arguments:
- queries: bfloat16 [64, 2, 8192], P('wide', None, 'kv'), may hold values from -14 to 14
- new_kv: bfloat16 [64, 2, 8, 256], P('wide', None, 'kv'), may hold values from -6 to 6
- suffix_cache: bfloat16 [64, 512, 8, 256], P('wide', None, 'kv'), may hold values from -14 to 14
- suffix_len: int32 [64], P('wide'), may hold values from 1 to 512, 24576 in all
- prefix_cache: bfloat16 [8192, 8, 256], P('wide', 'kv'), may hold values from -14 to 14
- prompt_len: int32 [8], replicated, may hold values from 1 to 1024, 4096 in all
- prompt_slot: int32 [8], replicated, may hold values from 0 to 7, each once
- sample_prompt: int32 [64, 1], replicated, may hold values from 0 to 7; in each aligned block of 4 rows (0 to 3, 4 to 7, ...) at most 2 rows name the same one
- out_weight: bfloat16 [8192, 8192], P('kv', 'wide'), may hold values from -0.0625 to 0.0625
Outputs:
- mixed: bfloat16 [64, 2, 8192], P('kv', None, 'wide')
Inputs may be any that keep to these rules, and one draw needn't show every extreme that they name: A permutation: prompt p's cache occupies rows prompt_slot[p] * 1024 to prompt_slot[p] * 1024 + 1023 of prefix_cache. `sample_prompt`: sample i is held by wide index i // 4; among the samples of one wide index at most 2 continue the same prompt.
All inputs are finite; a program needn't handle non-finite values. No bound on the sum of `suffix_len` on one device may be relied on, other than what follows from the above.
Results may differ from a plain program's by a relative error of at most 0.0061.
Values may be sent and summed in bfloat16 or wider, within the bound.
A program may use at most 64 MiB of HBM per device.

v0:
```python
import math

import jax
import jax.numpy as jnp
from jax import lax
from jax.sharding import PartitionSpec as P

HD = 128
GROUP = 8
STEPS = 2
PSH = 512
SUF = 512
NPROMPT = 8
MOST = 2


def sample_ranks(prompt_block):
    length = prompt_block.shape[-1]
    earlier = jnp.arange(length)[None, :] < jnp.arange(length)[:, None]
    matching = prompt_block[..., :, None] == prompt_block[..., None, :]
    return jnp.sum(matching & earlier, axis=-1)


def prefix_part(slots, prefix_cache, prompt_rows, segment):
    sources = slots.shape[0]
    item_count = slots.shape[1]
    kv_local = prefix_cache.shape[1]
    batch_rows = sources * item_count * STEPS
    scale = HD ** (-0.5)
    key_rows = prefix_cache[:, :, :HD]
    value_rows = prefix_cache[:, :, HD:]
    usable = segment * PSH + jnp.arange(PSH) < prompt_rows
    block_rows = math.gcd(batch_rows, max(1, 512 // (kv_local * GROUP)))

    def one_block(query_block):
        scores = (
            jnp.einsum("bgxd,jgd->bgxj", query_block, key_rows, preferred_element_type=jnp.float32)
            * scale
        )
        masked = jnp.where(usable, scores, -1e30)
        row_max = jnp.max(masked, axis=-1)
        weights = jnp.where(usable, jnp.exp(masked - row_max[..., None]), 0.0)
        row_sum = jnp.sum(weights, axis=-1)
        weights_bf = (weights / jnp.maximum(row_sum, 1.0)[..., None]).astype(jnp.bfloat16)
        result = jnp.einsum(
            "bgxj,jgd->bgxd", weights_bf, value_rows, preferred_element_type=jnp.float32
        )
        return (result.astype(jnp.bfloat16), row_max, row_sum)

    query_blocks = slots.reshape(batch_rows // block_rows, block_rows, kv_local, GROUP, HD)
    results = lax.map(one_block, query_blocks)
    part_out = results[0].reshape(sources, item_count, -1)
    part_max = results[1].reshape(sources, item_count, -1)
    part_sum = results[2].reshape(sources, item_count, -1)
    part_out = lax.all_to_all(part_out, "wide", split_axis=0, concat_axis=0, tiled=True)
    part_max, part_sum = (
        lax.all_to_all(part_max, "wide", split_axis=0, concat_axis=0, tiled=True),
        lax.all_to_all(part_sum, "wide", split_axis=0, concat_axis=0, tiled=True),
    )
    return (part_out, part_max, part_sum)


def per_device(
    queries,
    new_kv,
    suffix_cache,
    suffix_len,
    prefix_cache,
    prompt_len,
    prompt_slot,
    sample_prompt,
    out_weight,
):
    wide_count = lax.axis_size("wide")
    split_count = wide_count // NPROMPT
    position = lax.axis_index("wide")
    held_rows = queries.shape[0]
    kv_local = new_kv.shape[2]
    scale = HD ** (-0.5)
    prompt_ids = sample_prompt[:, 0]
    my_prompts = lax.dynamic_slice_in_dim(prompt_ids, position * held_rows, held_rows)
    prompt_range = jnp.arange(NPROMPT)
    slot_range = jnp.arange(MOST)
    my_group = jnp.sum(
        jnp.where(my_prompts[:, None] == prompt_range[None, :], prompt_slot[None, :], 0), axis=1
    )
    my_rank = sample_ranks(my_prompts)
    picked = (my_group[:, None, None] == prompt_range[None, :, None]) & (
        my_rank[:, None, None] == slot_range[None, None, :]
    )
    own_group = position // split_count
    segment = position % split_count
    owner_match = prompt_slot == own_group
    prompt_rows = jnp.sum(jnp.where(owner_match, prompt_len, 0))
    own_prompt = jnp.sum(jnp.where(owner_match, prompt_range, 0))
    flat_queries = queries.reshape(held_rows, -1)
    everyone = lax.all_gather(flat_queries, "wide", axis=0, tiled=True)
    blocks = prompt_ids.reshape(wide_count, held_rows)
    block_rank = sample_ranks(blocks)
    chosen = (blocks[:, :, None] == own_prompt) & (
        block_rank[:, :, None] == slot_range[None, None, :]
    )
    incoming = jnp.einsum(
        "hrc,hrx->hcx",
        chosen.astype(jnp.bfloat16),
        everyone.reshape(wide_count, held_rows, -1),
        preferred_element_type=jnp.float32,
    ).astype(jnp.bfloat16)
    part_out, part_max, part_sum = prefix_part(incoming, prefix_cache, prompt_rows, segment)
    picked_bf = picked.astype(jnp.bfloat16)
    picked_f32 = picked.astype(jnp.float32)
    prefix_out = jnp.einsum(
        "rgc,gscx->rsx",
        picked_bf,
        part_out.reshape(NPROMPT, split_count, MOST, -1),
        preferred_element_type=jnp.float32,
    )
    prefix_max = jnp.einsum(
        "rgc,gscy->rsy",
        picked_f32,
        part_max.reshape(NPROMPT, split_count, MOST, -1),
        precision=lax.Precision.HIGHEST,
    )
    prefix_sum = jnp.einsum(
        "rgc,gscy->rsy",
        picked_f32,
        part_sum.reshape(NPROMPT, split_count, MOST, -1),
        precision=lax.Precision.HIGHEST,
    )
    prefix_out = prefix_out.reshape(held_rows, split_count, STEPS, kv_local, GROUP, HD)
    prefix_max = prefix_max.reshape(held_rows, split_count, STEPS, kv_local, GROUP)
    prefix_sum = prefix_sum.reshape(held_rows, split_count, STEPS, kv_local, GROUP)
    query_rows = queries.reshape(held_rows, STEPS, kv_local, GROUP, HD)
    local_rows = jnp.concatenate([suffix_cache, new_kv], axis=1)
    local_scores = (
        jnp.einsum(
            "stgxd,sjgd->stgxj",
            query_rows,
            local_rows[..., :HD],
            preferred_element_type=jnp.float32,
        )
        * scale
    )
    positions = jnp.arange(SUF + STEPS)
    step_ids = jnp.arange(STEPS)
    local_ok = jnp.where(
        positions[None, None, :] < SUF,
        positions[None, None, :] < suffix_len[:, None, None],
        positions[None, None, :] - SUF <= step_ids[None, :, None],
    )
    local_ok = local_ok[:, :, None, None, :]
    local_masked = jnp.where(local_ok, local_scores, -1e30)
    local_max = jnp.max(local_masked, axis=-1)
    local_weights = jnp.where(local_ok, jnp.exp(local_masked - local_max[..., None]), 0.0)
    local_sum = jnp.sum(local_weights, axis=-1)
    local_bf = (local_weights / local_sum[..., None]).astype(jnp.bfloat16)
    local_out = jnp.einsum(
        "stgxj,sjgd->stgxd", local_bf, local_rows[..., HD:], preferred_element_type=jnp.float32
    )
    overall = jnp.maximum(jnp.max(prefix_max, axis=1), local_max)
    seg_weight = prefix_sum * jnp.exp(prefix_max - overall[:, None])
    local_weight = local_sum * jnp.exp(local_max - overall)
    numerator = (
        jnp.sum(seg_weight[..., None] * prefix_out, axis=1) + local_weight[..., None] * local_out
    )
    denominator = jnp.sum(seg_weight, axis=1) + local_weight
    attn = (numerator / denominator[..., None]).astype(jnp.bfloat16).reshape(held_rows, STEPS, -1)
    terms = jnp.einsum(
        "stk,kd->std",
        lax.all_gather(attn, "wide", axis=0, tiled=True),
        out_weight,
        preferred_element_type=jnp.float32,
    )
    summed = lax.psum_scatter(terms, "kv", scatter_dimension=0, tiled=True)
    return summed.astype(jnp.bfloat16)


def solution(mesh):
    return jax.shard_map(
        per_device,
        mesh=mesh,
        in_specs=(
            P("wide", None, "kv"),
            P("wide", None, "kv", None),
            P("wide", None, "kv", None),
            P("wide"),
            P("wide", "kv", None),
            P(),
            P(),
            P(),
            P("kv", "wide"),
        ),
        out_specs=P("kv", None, "wide"),
        check_vma=False,
    )
```

profile of v0, /device:TPU:0, one launch (start us, length us, event | category | flops | bytes accessed | tf_op | source)
XLA Modules:
  0.0 163.3 jit_solution(1750091661383867363)
XLA Ops:
  6.6 1.5 reshape.210
  8.1 0.9 reshape.206
  9.1 0.5 broadcast.139
  9.6 1.3 reduce.3
  11.3 1.6 fusion.47
  13.1 0.7 convert_reduce_fusion.1
  13.8 0.7 fusion.42
  14.6 0.6 broadcast_compare_fusion
  15.3 2.7 %copy_dynamic-update-slice_fusion.3 = bf16[4,514,4,256]{3,1,2,0:T(8,128)(2,1)S(1)} fusion(bf16[4,512,4,256]{3,2,1,0:T(4,128)(2,1)} %param.13), kind=kLoop, calls=%fused_computation.23 | loop fusion | bytes 8388608
  18.1 2.0 %copy-done = bf16[4,514,4,256]{3,1,2,0:T(8,128)(2,1)} copy-done((bf16[4,514,4,256]{3,1,2,0:T(8,128)(2,1)}, bf16[4,514,4,256]{3,1,2,0:T(8,128)(2,1)S(1)}, u32[]{:S(2)}) %copy-start) | copy-done | bytes 4210712
  20.1 0.8 fusion.48
  20.8 29.4 %all-gather.6.cloned.1.call-done = bf16[16,4,8192]{2,1,0:T(4,128)(2,1)} async-done(((bf16[1,4,8192]{2,1,0:T(4,128)(2,1)}), bf16[16,4,8192]{2,1,0:T(4,128)(2,1)}) %all-gather.6.cloned.1.call-update) | async-done | bytes 1048592 | tf_op jit(solution)/shard_map/all_gather | solution.py:97
  50.2 1.9 %convolution_convert_fusion.1 = bf16[16,2,8192]{2,1,0:T(2,128)(2,1)S(1)} fusion(bf16[16,4,8192]{2,1,0:T(4,128)(2,1)} %all-gather.6.cloned.1.call-done, pred[16,4]{1,0:T(8,128)(4,1)S(1)} %broadcast_compare_fusion, s32[16,4]{1,0:T(8,128)S(1)} %copy.93), kind=kOutput, calls=%fused_computation.20 | convolution fusion | flops 2359552 | bytes 1573184 | tf_op jit(solution)/shard_map/hrc,hrx->hcx/dot_general | solution.py:103
  52.1 0.4 reshape.201
  52.6 7.7 %while.15 = (s32[]{:T(128)}, bf16[4,16,4,8,128]{4,3,2,1,0:T(8,128)(2,1)S(1)}, f32[4,16,4,8]{3,2,1,0:T(4,128)S(1)}, f32[4,16,4,8]{3,2,1,0:T(4,128)S(1)}, bf16[4,1...) while((s32[]{:T(128)}, ...), condition=%wide.region_8.9_spmd.clone, body=%wide.region_5.8_spmd.clone.sunk | while | flops 136905216 | bytes 4866177 | solution.py:51
  52.6 0.7 add_compare_fusion.2
  53.3 0.4 fusion.57
  53.7 0.3 fusion.58
  54.0 0.4 fusion.59
  54.5 0.7 add_compare_fusion.2
  55.2 0.4 fusion.57
  56.0 0.4 fusion.59
  56.5 0.7 add_compare_fusion.2
  57.2 0.4 fusion.57
  57.9 0.4 fusion.59
  58.4 0.7 add_compare_fusion.2
  59.1 0.4 fusion.57
  59.8 0.4 fusion.59
  60.5 0.7 reshape.235
  61.1 3.6 %all-to-all-start.1 = ((f32[16,1,128]{2,1,0:T(1,128)}), f32[16,1,128]{2,1,0:T(1,128)S(1)}, u32[]{:S(2)}, u32[]{:S(2)}) async-start(f32[16,1,128]{2,1,0:T(1,128)} %reshape.235), calls=%async_computation.1 | async-start | bytes 16384 | tf_op jit(solution)/shard_map/all_to_all | solution.py:57
  64.9 0.7 reshape.233
  65.6 5.5 %all-to-all-done.1 = f32[16,1,128]{2,1,0:T(1,128)S(1)} async-done(((f32[16,1,128]{2,1,0:T(1,128)}), f32[16,1,128]{2,1,0:T(1,128)S(1)}, u32[]{:S(2)}, u32[]{:S(2)}) %all-to-all-start.1) | async-done | bytes 8224 | tf_op jit(solution)/shard_map/all_to_all | solution.py:57
  71.1 3.5 %all-to-all-start = ((f32[16,1,128]{2,1,0:T(1,128)}), f32[16,1,128]{2,1,0:T(1,128)S(1)}, u32[]{:S(2)}, u32[]{:S(2)}) async-start(f32[16,1,128]{2,1,0:T(1,128)} %reshape.233), calls=%async_computation | async-start | bytes 16384 | tf_op jit(solution)/shard_map/all_to_all | solution.py:58
  74.8 0.9 reshape.207
  75.7 5.2 %all-to-all-done = f32[16,1,128]{2,1,0:T(1,128)S(1)} async-done(((f32[16,1,128]{2,1,0:T(1,128)}), f32[16,1,128]{2,1,0:T(1,128)S(1)}, u32[]{:S(2)}, u32[]{:S(2)}) %all-to-all-start) | async-done | bytes 8224 | tf_op jit(solution)/shard_map/all_to_all | solution.py:58
  81.0 3.6 %all-to-all-start.2 = ((bf16[16,2,8192]{2,1,0:T(2,128)(2,1)}), bf16[16,2,8192]{2,1,0:T(2,128)(2,1)S(1)}, u32[]{:S(2)}, u32[]{:S(2)}) async-start(bf16[16,2,8192]{2,1,0:T(2,128)(2,1)} %reshape.207), calls=%async_computation.2 | async-start | bytes 1048576 | tf_op jit(solution)/shard_map/all_to_all | solution.py:55
  84.9 0.5 broadcast.140
  85.5 0.7 reduce.4
  86.4 0.7 reduce.5
  88.1 10.8 %all-to-all-done.2 = bf16[16,2,8192]{2,1,0:T(2,128)(2,1)S(1)} async-done(((bf16[16,2,8192]{2,1,0:T(2,128)(2,1)}), bf16[16,2,8192]{2,1,0:T(2,128)(2,1)S(1)}, u32[]{:S(2)}, u32[]{:S(2)}) %all-to-all-start.2) | async-done | bytes 524320 | tf_op jit(solution)/shard_map/all_to_all | solution.py:55
  99.4 0.6 fusion.18
  99.9 2.1 %fusion.23 = bf16[4,2,4,8,128]{4,3,1,2,0:T(8,128)(2,1)S(1)} fusion(bf16[4,514,4,256]{3,1,2,0:T(8,128)(2,1)} %copy-done, f32[4,2,4,8,514]{4,3,1,2,0:T(8,128)S(1)} %get-tuple-element.148, f32[4,2,4,8]{3,1,2,0:T(2,128)S(1)} %fusion.26, f32[4,2,4,8]{3,1,2,0:T(2,128)S(1)} %get-tuple-element.147, pred[4,2,514]{2,1,0:T(4,128)(4,1)S(1)} %copy-done.2, ...), kind=kOutput, calls=%fused_computation.38 | convolution fusion | flops 34342912 | bytes 2861072 | tf_op jit(solution)/shard_map/stgxj,sjgd->stgxd/dot_general | solution.py:157
  102.1 0.6 reshape.209
  102.8 37.4 %all-gather.4.cloned.1.call-done = bf16[64,2,4096]{2,1,0:T(2,128)(2,1)} async-done(((bf16[4,2,4096]{2,1,0:T(2,128)(2,1)}), bf16[64,2,4096]{2,1,0:T(2,128)(2,1)}) %all-gather.4.cloned.1.call-update) | async-done | bytes 1048592 | tf_op jit(solution)/shard_map/all_gather | solution.py:170
  140.1 4.3 %fusion.10 = f32[64,2,512]{2,0,1:T(8,128)} fusion(bf16[4096,512]{1,0:T(8,128)(2,1)} %param.19, bf16[64,2,4096]{2,1,0:T(2,128)(2,1)} %all-gather.4.cloned.1.call-done), kind=kOutput, calls=%fused_computation.21 | convolution fusion | flops 536870912 | bytes 5505024 | tf_op jit(solution)/shard_map/stk,kd->std/dot_general | solution.py:168
  144.4 10.7 %reduce-scatter.2.cloned.1.call-done = f32[32,2,512]{2,0,1:T(8,128)} async-done(((f32[64,2,512]{2,0,1:T(8,128)}), f32[32,2,512]{2,0,1:T(8,128)}) %reduce-scatter.2.cloned.1.call-update) | async-done | bytes 131088 | tf_op jit(solution)/shard_map/reduce_scatter | solution.py:174
  155.2 0.9 convert_element_type.35
  156.1 0.7 copy.118
  (83 shorter events, 4.8 us)
Async XLA Ops:
  6.5 6.5 %copy-start.8 = (s32[64,1]{0,1:T(1,128)S(1)}, s32[64,1]{0,1:T(1,128)}, u32[]{:S(2)}) copy-start(s32[64,1]{0,1:T(1,128)} %param.18) | copy-start | bytes 772
  6.5 7.3 %copy-start.4 = (s32[8]{0:T(128)S(1)}, s32[8]{0:T(128)}, u32[]{:S(2)}) copy-start(s32[8]{0:T(128)} %param.16) | copy-start | bytes 100
  6.5 7.3 %copy-start.5 = (s32[8]{0:T(128)S(1)}, s32[8]{0:T(128)}, u32[]{:S(2)}) copy-start(s32[8]{0:T(128)} %param.17) | copy-start | bytes 100
  6.5 8.0 %copy-start.7 = (s32[4]{0:T(128)S(1)}, s32[4]{0:T(128)}, u32[]{:S(2)}) copy-start(s32[4]{0:T(128)} %param.14) | copy-start | bytes 52
  6.5 43.7 %all-gather.6.cloned.1.call-start = ((), (), s32[]{:S(2)}) async-start(), calls=%async_computation.6 | async-start | bytes 1114112 | tf_op jit(solution)/shard_map/all_gather | solution.py:97
  13.1 1.5 copy-start.9
  15.3 2.8 %copy-start.1 = (pred[4,2,514]{2,1,0:T(4,128)(4,1)}, pred[4,2,514]{2,1,0:T(4,128)(4,1)S(1)}, u32[]{:S(2)}) copy-start(pred[4,2,514]{2,1,0:T(4,128)(4,1)S(1)} %broadcast_select_fusion) | copy-start | bytes 12340
  15.3 2.8 %copy-start.3 = (bf16[4,2,4,256]{3,2,1,0:T(4,128)(2,1)S(1)}, bf16[4,2,4,256]{3,2,1,0:T(4,128)(2,1)}, u32[]{:S(2)}) copy-start(bf16[4,2,4,256]{3,2,1,0:T(4,128)(2,1)} %param.12) | copy-start | bytes 49156
  18.1 2.0 %copy-start = (bf16[4,514,4,256]{3,1,2,0:T(8,128)(2,1)}, bf16[4,514,4,256]{3,1,2,0:T(8,128)(2,1)S(1)}, u32[]{:S(2)}) copy-start(bf16[4,514,4,256]{3,1,2,0:T(8,128)(2,1)S(1)} %copy_dynamic-update-slice_fusion.4) | copy-start | bytes 12632068
  52.5 12.2 %copy-start.11 = (s32[4]{0:T(128)S(1)}, s32[4]{0:T(128)}, u32[]{:S(2)}) copy-start(s32[4]{0:T(128)} %convert_reduce_fusion.1) | copy-start | bytes 52
  52.5 22.0 %copy-start.6 = (s32[8]{0:T(128)S(1)}, s32[8]{0:T(128)}, u32[]{:S(2)}) copy-start(s32[8]{0:T(128)} %param.17) | copy-start | bytes 100
  52.6 22.0 %copy-start.10 = (s32[4]{0:T(128)S(1)}, s32[4]{0:T(128)}, u32[]{:S(2)}) copy-start(s32[4]{0:T(128)} %copy-done.9) | copy-start | bytes 52
  52.6 32.1 %copy-start.2 = (pred[4,2,514]{2,1,0:T(4,128)(4,1)S(1)}, pred[4,2,514]{2,1,0:T(4,128)(4,1)}, u32[]{:S(2)}) copy-start(pred[4,2,514]{2,1,0:T(4,128)(4,1)} %copy-done.1) | copy-start | bytes 12340
  61.1 10.0 %all-to-all-start.1 = ((f32[16,1,128]{2,1,0:T(1,128)}), f32[16,1,128]{2,1,0:T(1,128)S(1)}, u32[]{:S(2)}, u32[]{:S(2)}) async-start(f32[16,1,128]{2,1,0:T(1,128)} %reshape.235), calls=%async_computation.1 | async-start | bytes 16384 | tf_op jit(solution)/shard_map/all_to_all | solution.py:57
  71.1 9.8 %all-to-all-start = ((f32[16,1,128]{2,1,0:T(1,128)}), f32[16,1,128]{2,1,0:T(1,128)S(1)}, u32[]{:S(2)}, u32[]{:S(2)}) async-start(f32[16,1,128]{2,1,0:T(1,128)} %reshape.233), calls=%async_computation | async-start | bytes 16384 | tf_op jit(solution)/shard_map/all_to_all | solution.py:58
  81.0 18.0 %all-to-all-start.2 = ((bf16[16,2,8192]{2,1,0:T(2,128)(2,1)}), bf16[16,2,8192]{2,1,0:T(2,128)(2,1)S(1)}, u32[]{:S(2)}, u32[]{:S(2)}) async-start(bf16[16,2,8192]{2,1,0:T(2,128)(2,1)} %reshape.207), calls=%async_computation.2 | async-start | bytes 1048576 | tf_op jit(solution)/shard_map/all_to_all | solution.py:55
  84.5 55.6 %all-gather.4.cloned.1.call-start = ((), (), s32[]{:S(2)}) async-start(), calls=%async_computation.4 | async-start | bytes 1114112 | tf_op jit(solution)/shard_map/all_gather | solution.py:170
  102.7 52.5 %reduce-scatter.2.cloned.1.call-start = ((), (), s32[]{:S(2)}) async-start(), calls=%async_computation.5 | async-start | bytes 393216 | tf_op jit(solution)/shard_map/reduce_scatter | solution.py:174
Sparse Core Ops, SparseCore 0:
  9.5 40.6 all-gather.5
  102.8 37.2 all-gather.3
  144.6 10.5 reduce-scatter.1
where the time goes:
time: 164 us; the launch traced here: 163 us
  waiting for transfers between devices  99.1 us (60%)
  local copies, waits for them, and re-layouts  16 us (10%)
  between operations  13.5 us (8%)
  matrix products  13.3 us (8%)
  starting transfers between devices  10.8 us (7%)
  other arithmetic  10.4 us (6%)
    all_gather x1, waiting for transfers between devices, per_device(): lax.all_gather(attn, 'wide', axis=0, tiled=True)  37.4 us
    all_gather x1, waiting for transfers between devices, per_device(): everyone = lax.all_gather(flat_queries, 'wide', axis=0, tiled=True)  29.4 us
    all_to_all x1, waiting for transfers between devices, prefix_part(): lax.all_to_all(part_out, 'wide', split_axis=0, concat_axis=0, tiled=True)  10.8 us
    reduce_scatter x1, waiting for transfers between devices, per_device(): summed = lax.psum_scatter(terms, 'kv', scatter_dimension=0, tiled=True)  10.7 us
    unnamed x34, local copies, waits for them, and re-layouts  8.6 us
    all_to_all x1, waiting for transfers between devices, prefix_part(): lax.all_to_all(part_max, 'wide', split_axis=0, concat_axis=0, tiled=True)  5.48 us
    all_to_all x1, waiting for transfers between devices, prefix_part(): lax.all_to_all(part_sum, 'wide', split_axis=0, concat_axis=0, tiled=True)  5.24 us
    dot_general x1, matrix products, per_device(): jnp.einsum('stk,kd->std', lax.all_gather(attn, 'wide', axis=0, tiled=True...  4.26 us
  transfers between devices with their start and end apart: 6, of which 6 were waited for; matrix products, arithmetic and copies ran while one was open for 10% of the time, Pallas kernels for 0%

commit v1 on v0

--- a/solution.py
+++ b/solution.py
@@ -1,8 +1,11 @@
+import functools
 import math
 
 import jax
 import jax.numpy as jnp
 from jax import lax
+from jax.experimental import pallas as pl
+from jax.experimental.pallas import tpu as pltpu
 from jax.sharding import PartitionSpec as P
 
 HD = 128
@@ -60,7 +63,7 @@
     return (part_out, part_max, part_sum)
 
 
-def per_device(
+def general_device(
     queries,
     new_kv,
     suffix_cache,
@@ -175,9 +178,476 @@
     return summed.astype(jnp.bfloat16)
 
 
+MESH = pl.DeviceIdType.MESH
+CHIPS = 8
+HELD = 4
+KVL = 4
+ROWS = STEPS * GROUP
+SPAN = KVL * ROWS
+LOCAL = SUF + 128
+SCALE = HD ** (-0.5)
+NT = (((1,), (1,)), ((), ()))
+
+
+def fused_kernel(
+    slen_ref,
+    plen_ref,
+    pslot_ref,
+    sprompt_ref,
+    q_ref,
+    new_ref,
+    suf_hbm,
+    pre_hbm,
+    w_hbm,
+    o_ref,
+    suf,
+    pre,
+    w,
+    split_p,
+    turn_p,
+    lkv,
+    pkv,
+    qslot,
+    qrecv,
+    lo,
+    lm,
+    ll,
+    half_o,
+    half_m,
+    half_l,
+    so_send,
+    st_send,
+    so_recv,
+    st_recv,
+    co_send,
+    cs_send,
+    co_recv,
+    cs_recv,
+    ag,
+    lhs,
+    terms,
+    y_send,
+    y_recv,
+    loc_sem,
+    q_ss,
+    q_rs,
+    qf_ss,
+    qf_rs,
+    x_ss,
+    x_rs,
+    c_ss,
+    c_rs,
+    s_ss,
+    s_rs,
+    z_ss,
+    z_rs,
+    ax_ss,
+    ax_rs,
+    ac_ss,
+    ac_rs,
+    y_ss,
+    y_rs,
+):
+    f32, bf16 = jnp.float32, jnp.bfloat16
+    wide = lax.axis_index("wide")
+    y = lax.axis_index("kv")
+    chip = wide // 2
+    core = wide % 2
+    zc = chip // 2
+    xc = chip % 2
+    sibling = (chip * 2 + 1 - core, y)
+
+    def at_chip(c):
+        return (c * 2 + core, y)
+
+    local_copies = [pltpu.make_async_copy(pre_hbm, pre, loc_sem.at[0])]
+    local_copies += [
+        pltpu.make_async_copy(suf_hbm.at[s], suf.at[s], loc_sem.at[1 + s]) for s in range(HELD)
+    ]
+    local_copies.append(pltpu.make_async_copy(w_hbm, w, loc_sem.at[1 + HELD]))
+    for copy in local_copies:
+        copy.start()
+
+    barrier = pltpu.get_barrier_semaphore()
+    for d in range(1, CHIPS):
+        pl.semaphore_signal(
+            barrier, inc=1, device_id=at_chip((chip + d) % CHIPS), device_id_type=MESH
+        )
+    pl.semaphore_signal(barrier, inc=1, device_id=sibling, device_id_type=MESH)
+    pl.semaphore_signal(barrier, inc=1, device_id=(wide, 1 - y), device_id_type=MESH)
+
+    prompts = [sprompt_ref[wide * HELD + s] for s in range(HELD)]
+    groups = [pslot_ref[p] for p in prompts]
+    ranks = []
+    for s in range(HELD):
+        rank = jnp.int32(0)
+        for e in range(s):
+            rank = rank + jnp.where(prompts[e] == prompts[s], 1, 0)
+        ranks.append(rank)
+    for c in range(CHIPS):
+        for m in range(MOST):
+            pick = jnp.int32(0)
+            for s in range(1, HELD):
+                pick = pick + jnp.where((groups[s] == c) & (ranks[s] == m), s, 0)
+            qslot[c, m * SPAN : (m + 1) * SPAN, :] = q_ref[pick]
+    prompt_rows = jnp.int32(0)
+    for p in range(NPROMPT):
+        prompt_rows = prompt_rows + jnp.where(pslot_ref[p] == chip, plen_ref[p], 0)
+
+    out_row = lax.broadcasted_iota(jnp.int32, (256, 256), 0)
+    in_row = lax.broadcasted_iota(jnp.int32, (256, 256), 1)
+    split_p[...] = jnp.where(in_row == (out_row & 31) * 8 + (out_row >> 5), 1.0, 0.0).astype(bf16)
+    source = (
+        ((out_row >> 1) & 3) * 64 + (out_row >> 6) * 16 + (out_row & 1) * 8 + ((out_row >> 3) & 7)
+    )
+    turn_p[...] = jnp.where(in_row == source, 1.0, 0.0).astype(bf16)
+
+    pl.semaphore_wait(barrier, CHIPS + 1)
+
+    q_copies = {}
+    for d in (4, 3, 5, 2, 6, 1, 7):
+        dst = (chip + d) % CHIPS
+        q_copies[d] = pltpu.make_async_remote_copy(
+            src_ref=qslot.at[dst],
+            dst_ref=qrecv.at[core, chip],
+            send_sem=q_ss.at[d],
+            recv_sem=q_rs.at[d],
+            device_id=at_chip(dst),
+            device_id_type=MESH,
+        )
+        q_copies[d].start()
+    qrecv[core, chip] = qslot[chip]
+    forwards = {}
+
+    def forward(d):
+        src = (chip + CHIPS - d) % CHIPS
+        if d:
+            q_copies[d].wait_recv()
+        forwards[d] = pltpu.make_async_remote_copy(
+            src_ref=qrecv.at[core, src],
+            dst_ref=qrecv.at[core, src],
+            send_sem=qf_ss.at[d],
+            recv_sem=qf_rs.at[d],
+            device_id=sibling,
+            device_id_type=MESH,
+        )
+        forwards[d].start()
+
+    forward(0)
+
+    def split_heads(src, dst):
+        def step(i, carry):
+            first = pl.multiple_of(i * 512, 512)
+            rows = jnp.concatenate(
+                [src[pl.ds(first, 256), :], src[pl.ds(first + 256, 256), :]], axis=1
+            )
+            parted = jnp.dot(split_p[...], rows, preferred_element_type=f32).astype(bf16)
+            to = pl.multiple_of(i * 64, 64)
+            for k in range(8):
+                dst[k, pl.ds(to, 32), :] = parted[k * 32 : (k + 1) * 32, :HD]
+                dst[k, pl.ds(to + 32, 32), :] = parted[k * 32 : (k + 1) * 32, HD:]
+            return carry
+
+        lax.fori_loop(0, 8, step, 0)
+
+    local_copies[0].wait()
+    split_heads(pre, pkv)
+
+    lkv[:, SUF:, :] = jnp.zeros((8, LOCAL - SUF, HD), bf16)
+    col = lax.broadcasted_iota(jnp.int32, (ROWS, LOCAL), 1)
+    step_of = lax.broadcasted_iota(jnp.int32, (ROWS, LOCAL), 0) // GROUP
+
+    def local_part(s):
+        local_copies[1 + s].wait()
+        split_heads(suf.at[s], lkv)
+        lkv[:, SUF : SUF + 16, :] = new_ref[s]
+        limit = jnp.where(col < SUF, slen_ref[s], SUF + 1 + step_of)
+        ok = col < limit
+        for g in range(KVL):
+            query = q_ref[s, g * ROWS : (g + 1) * ROWS, :]
+            scores = lax.dot_general(query, lkv[g], NT, preferred_element_type=f32) * SCALE
+            masked = jnp.where(ok, scores, -1e30)
+            top = jnp.max(masked, axis=1, keepdims=True)
+            weights = jnp.where(ok, jnp.exp(masked - top), 0.0)
+            total = jnp.sum(weights, axis=1, keepdims=True)
+            result = jnp.dot(weights.astype(bf16), lkv[KVL + g], preferred_element_type=f32)
+            here = slice(g * ROWS, (g + 1) * ROWS)
+            lo[s, here, :] = result
+            lm[s, here, :] = jnp.broadcast_to(top, (ROWS, HD))
+            ll[s, here, :] = jnp.broadcast_to(total, (ROWS, HD))
+
+    local_part(0)
+    forward(1)
+    forward(7)
+    local_part(1)
+    forward(2)
+    forward(6)
+    local_part(2)
+    for d in (3, 5, 4):
+        forward(d)
+    local_part(3)
+
+    usable = lax.broadcasted_iota(jnp.int32, (256, PSH), 1) < prompt_rows - core * PSH
+
+    def prefix_half(which):
+        for g in range(KVL):
+            query = qrecv[which, :, :, :].reshape(CHIPS, MOST, KVL, ROWS, HD)[:, :, g]
+            query = query.reshape(256, HD)
+            scores = lax.dot_general(query, pkv[g], NT, preferred_element_type=f32) * SCALE
+            masked = jnp.where(usable, scores, -1e30)
+            top = jnp.max(masked, axis=1, keepdims=True)
+            weights = jnp.where(usable, jnp.exp(masked - top), 0.0)
+            total = jnp.sum(weights, axis=1, keepdims=True)
+            result = jnp.dot(weights.astype(bf16), pkv[KVL + g], preferred_element_type=f32)
+            shape = (CHIPS, MOST, ROWS, HD)
+            half_o[:, :, g] = result.reshape(shape)
+            half_m[:, :, g] = jnp.broadcast_to(top, (256, HD)).reshape(shape)
+            half_l[:, :, g] = jnp.broadcast_to(total, (256, HD)).reshape(shape)
+
+    sub = lax.broadcasted_iota(jnp.int32, (8, HD), 0)
+
+    def stat_rows(top, total):
+        return jnp.where(sub == 0, top.T[:8], total.T[:8])
+
+    for d in (0, 1, 2, 3, 4, 5, 6, 7):
+        forwards[d].wait_recv()
+    prefix_half(1 - core)
+
+    def pack_half(c, carry):
+        so_send[c] = half_o[c].reshape(128, HD).astype(bf16)
+        st_send[c] = stat_rows(half_m[c].reshape(128, HD), half_l[c].reshape(128, HD))
+        return carry
+
+    lax.fori_loop(0, CHIPS, pack_half, 0)
+    swaps = []
+    for i, (src, dst) in enumerate(((so_send, so_recv), (st_send, st_recv))):
+        copy = pltpu.make_async_remote_copy(
+            src_ref=src,
+            dst_ref=dst,
+            send_sem=x_ss.at[i],
+            recv_sem=x_rs.at[i],
+            device_id=sibling,
+            device_id_type=MESH,
+        )
+        copy.start()
+        swaps.append(copy)
+    prefix_half(core)
+    for copy in swaps:
+        copy.wait_recv()
+
+    results = []
+
+    def merge(c):
+        m1, l1 = half_m[c].reshape(128, HD), half_l[c].reshape(128, HD)
+        other = st_recv[c]
+        m2 = jnp.broadcast_to(other[0:1], (HD, HD)).T
+        l2 = jnp.broadcast_to(other[1:2], (HD, HD)).T
+        top = jnp.maximum(m1, m2)
+        w1, w2 = jnp.exp(m1 - top), jnp.exp(m2 - top)
+        total = w1 * l1 + w2 * l2
+        mixed = w1 * half_o[c].reshape(128, HD) + w2 * so_recv[c].astype(f32)
+        return (mixed / total).astype(bf16), stat_rows(top, total)
+
+    for d in (4, 3, 5, 2, 6, 1, 7):
+        dst = (chip + d) % CHIPS
+        co_send[dst], cs_send[dst] = merge(dst)
+        for src, target, ss, rs in (
+            (co_send, co_recv, c_ss, c_rs),
+            (cs_send, cs_recv, s_ss, s_rs),
+        ):
+            copy = pltpu.make_async_remote_copy(
+                src_ref=src.at[dst],
+                dst_ref=target.at[chip],
+                send_sem=ss.at[d],
+                recv_sem=rs.at[d],
+                device_id=at_chip(dst),
+                device_id_type=MESH,
+            )
+            copy.start()
+            results.append(copy)
+    co_recv[chip], cs_recv[chip] = merge(chip)
+    for copy in results:
+        copy.wait_recv()
+
+    parts = []
+    for s in range(HELD):
+        stats = cs_recv[groups[s]]
+        block = co_recv[groups[s]].astype(f32)
+        first = jnp.broadcast_to(ranks[s] == 0, (SPAN, HD))
+        tops = jnp.broadcast_to(stats[0:1], (HD, HD)).T
+        totals = jnp.broadcast_to(stats[1:2], (HD, HD)).T
+        pm = jnp.where(first, tops[:SPAN], tops[SPAN:])
+        pt = jnp.where(first, totals[:SPAN], totals[SPAN:])
+        po = jnp.where(first, block[:SPAN], block[SPAN:])
+        overall = jnp.maximum(pm, lm[s])
+        wp = pt * jnp.exp(pm - overall)
+        wl = jnp.exp(lm[s] - overall)
+        parts.append(((wp * po + wl * lo[s]) / (wp + wl * ll[s])).astype(bf16))
+    attn = jnp.concatenate(parts, axis=0)
+    ag[wide] = jnp.dot(turn_p[...], attn, preferred_element_type=f32).astype(bf16)
+
+    sends = []
+
+    def push(index, ss, rs, device):
+        copy = pltpu.make_async_remote_copy(
+            src_ref=ag.at[index],
+            dst_ref=ag.at[index],
+            send_sem=ss,
+            recv_sem=rs,
+            device_id=device,
+            device_id_type=MESH,
+        )
+        copy.start()
+        sends.append(copy)
+        return copy
+
+    x_peer = at_chip(zc * 2 + 1 - xc)
+    z_in = {}
+    for d in (2, 1, 3):
+        z_in[d] = push(wide, z_ss.at[d], z_rs.at[d], at_chip(((zc + d) % 4) * 2 + xc))
+    x_in = {0: push(wide, ax_ss.at[0], ax_rs.at[0], x_peer)}
+    c_in = [push(wide, ac_ss.at[0], ac_rs.at[0], sibling)]
+
+    def pass_x(d):
+        x_in[d].wait_recv()
+        index = (((zc + 4 - d) % 4) * 2 + 1 - xc) * 2 + core
+        c_in.append(push(index, ac_ss.at[4 + d], ac_rs.at[4 + d], sibling))
+
+    def pass_z(d):
+        z_in[d].wait_recv()
+        index = (((zc + 4 - d) % 4) * 2 + xc) * 2 + core
+        x_in[d] = push(index, ax_ss.at[d], ax_rs.at[d], x_peer)
+        c_in.append(push(index, ac_ss.at[d], ac_rs.at[d], sibling))
+
+    for d in (1, 3, 2):
+        pass_z(d)
+    for d in (0, 1, 3, 2):
+        pass_x(d)
+    local_copies[1 + HELD].wait()
+    for copy in c_in:
+        copy.wait_recv()
+
+    for k in range(16):
+        block = ag[:, k * 16 : (k + 1) * 16, :].astype(f32)
+        lhs[:, k * 256 : k * 256 + 128] = block[:, :8].reshape(128, HD).astype(bf16)
+        lhs[:, k * 256 + 128 : (k + 1) * 256] = block[:, 8:].reshape(128, HD).astype(bf16)
+
+    theirs = pl.multiple_of((1 - y) * 64, 64)
+    mine = pl.multiple_of(y * 64, 64)
+    y_copies = []
+    for n in range(2):
+        terms[n] = jnp.dot(
+            lhs[...], w[:, n * 256 : (n + 1) * 256], preferred_element_type=f32
+        )
+        y_send[n] = terms[n, pl.ds(theirs, 64), :].astype(bf16)
+        copy = pltpu.make_async_remote_copy(
+            src_ref=y_send.at[n],
+            dst_ref=y_recv.at[n],
+            send_sem=y_ss.at[n],
+            recv_sem=y_rs.at[n],
+            device_id=(wide, 1 - y),
+            device_id_type=MESH,
+        )
+        copy.start()
+        y_copies.append(copy)
+    for n in range(2):
+        y_copies[n].wait_recv()
+        total = terms[n, pl.ds(mine, 64), :] + y_recv[n].astype(f32)
+        o_ref[:, n * 256 : (n + 1) * 256] = total.astype(bf16)
+
+    for copy in [*q_copies.values(), *forwards.values(), *swaps, *results, *sends, *y_copies]:
+        copy.wait_send()
+
+
+def fused_device(
+    queries,
+    new_kv,
+    suffix_cache,
+    suffix_len,
+    prefix_cache,
+    prompt_len,
+    prompt_slot,
+    sample_prompt,
+    out_weight,
+):
+    f32, bf16 = jnp.float32, jnp.bfloat16
+    q_rows = queries.reshape(HELD, STEPS, KVL, GROUP, HD).transpose(0, 2, 1, 3, 4)
+    q_rows = q_rows.reshape(HELD, SPAN, HD)
+    new_rows = new_kv.reshape(HELD, STEPS, KVL, 2, HD).transpose(0, 3, 2, 1, 4)
+    new_rows = jnp.pad(
+        new_rows.reshape(HELD, 2 * KVL, STEPS, HD), ((0, 0), (0, 0), (0, 16 - STEPS), (0, 0))
+    )
+    suf = suffix_cache.reshape(HELD, SUF, KVL, 2, HD).transpose(0, 1, 3, 2, 4)
+    suf = suf.reshape(HELD, SUF * 8, HD)
+    pre = prefix_cache.reshape(PSH, KVL, 2, HD).transpose(0, 2, 1, 3).reshape(PSH * 8, HD)
+    vm, sm, hbm = pltpu.VMEM, pltpu.SMEM, pl.ANY
+    dma = pltpu.SemaphoreType.DMA
+    half = (CHIPS, MOST, KVL, ROWS, HD)
+    scratch = [
+        vm((HELD, SUF * 8, HD), bf16),
+        vm((PSH * 8, HD), bf16),
+        vm((KVL * 1024, 512), bf16),
+        vm((256, 256), bf16),
+        vm((256, 256), bf16),
+        vm((8, LOCAL, HD), bf16),
+        vm((8, PSH, HD), bf16),
+        vm((CHIPS, 128, HD), bf16),
+        vm((2, CHIPS, 128, HD), bf16),
+        vm((HELD, SPAN, HD), f32),
+        vm((HELD, SPAN, HD), f32),
+        vm((HELD, SPAN, HD), f32),
+        vm(half, f32),
+        vm(half, f32),
+        vm(half, f32),
+        vm((CHIPS, 128, HD), bf16),
+        vm((CHIPS, 8, HD), f32),
+        vm((CHIPS, 128, HD), bf16),
+        vm((CHIPS, 8, HD), f32),
+        vm((CHIPS, 128, HD), bf16),
+        vm((CHIPS, 8, HD), f32),
+        vm((CHIPS, 128, HD), bf16),
+        vm((CHIPS, 8, HD), f32),
+        vm((16, 256, HD), bf16),
+        vm((128, 4096), bf16),
+        vm((2, 128, 256), f32),
+        vm((2, 64, 256), bf16),
+        vm((2, 64, 256), bf16),
+        dma((2 + HELD,)),
+    ]
+    for count in (8, 8, 2, 8, 8, 4, 4, 8, 2):
+        scratch += [dma((count,)), dma((count,))]
+    out = pl.pallas_call(
+        fused_kernel,
+        out_shape=jax.ShapeDtypeStruct((64, 512), bf16),
+        in_specs=[pl.BlockSpec(memory_space=sm)] * 4
+        + [pl.BlockSpec(memory_space=vm)] * 2
+        + [pl.BlockSpec(memory_space=hbm)] * 3,
+        out_specs=pl.BlockSpec(memory_space=vm),
+        scratch_shapes=scratch,
+        compiler_params=pltpu.CompilerParams(
+            collective_id=0, has_side_effects=True, vmem_limit_bytes=56 * 1024 * 1024
+        ),
+        cost_estimate=pl.CostEstimate(
+            flops=4_000_000_000, bytes_accessed=12_000_000, transcendentals=1_500_000
+        ),
+    )(
+        suffix_len,
+        prompt_len,
+        prompt_slot,
+        sample_prompt.reshape(-1),
+        q_rows,
+        new_rows,
+        suf,
+        pre,
+        out_weight,
+    )
+    return out.reshape(32, STEPS, 512)
+
+
 def solution(mesh):
+    small = mesh.shape["wide"] == 2 * CHIPS and mesh.shape["kv"] == 2
     return jax.shard_map(
-        per_device,
+        fused_device if small else general_device,
         mesh=mesh,
         in_specs=(
             P("wide", None, "kv"),

time: 164 us -> 56.1 us (0.34)
  waiting for transfers between devices: 99.1 us -> 0 us
  Pallas kernels: 0 us -> 51.4 us
  between operations: 13.5 us -> 0.02 us
  matrix products: 13.3 us -> 0 us
  local copies, waits for them, and re-layouts: 16 us -> 4.44 us
  starting transfers between devices: 10.8 us -> 0 us
  other arithmetic: 10.4 us -> 0 us
    all_gather x2 -> x0, waiting for transfers between devices: 66.7 us -> none  [the longest x1 37.4 us: per_device(): lax.all_gather(attn, 'wide', axis=0, tiled=True)]
    pallas_call x0 -> x1, Pallas kernels: none -> 51.4 us  [fused_device(): pl.pallas_call(fused_kernel, out_shape=jax.ShapeDtypeStruct((64, 512), bf...]
    all_to_all x3 -> x0, waiting for transfers between devices: 21.5 us -> none  [the longest x1 10.8 us: prefix_part(): lax.all_to_all(part_out, 'wide', split_axis=0, concat_axis=0, tiled=True)]
    dot_general x15 -> x0, matrix products: 13.3 us -> none  [the longest x1 4.26 us: per_device(): jnp.einsum('stk,kd->std', lax.all_gather(attn, 'wide', axis=0, tiled=True...]
    reduce_scatter x1 -> x0, waiting for transfers between devices: 10.7 us -> none  [per_device(): summed = lax.psum_scatter(terms, 'kv', scatter_dimension=0, tiled=True)]
    all_to_all x3 -> x0, starting transfers between devices: 10.7 us -> none  [the longest x1 3.62 us: prefix_part(): lax.all_to_all(part_max, 'wide', split_axis=0, concat_axis=0, tiled=True)]
    unnamed x34 -> x0, local copies, waits for them, and re-layouts: 8.6 us -> none
    reduce_sum x9 -> x0, other arithmetic: 3.27 us -> none  [the longest x4 1.3 us: one_block(): row_sum = jnp.sum(weights, axis=-1)]
  transfers between devices with their start and end apart: 6 -> 0, of which waited for: 6 -> 0; matrix products, arithmetic and copies ran while one was open for 10% -> 0% of each run, Pallas kernels for 0% -> 0%
where the time goes in v1:
time: 56.1 us; the launch traced here: 55.8 us
  Pallas kernels  51.4 us (92%)
  local copies, waits for them, and re-layouts  4.44 us (8%)
    pallas_call x1, Pallas kernels, fused_device(): pl.pallas_call(fused_kernel, out_shape=jax.ShapeDtypeStruct((64, 512), bf...  51.4 us
    reshape x2, local copies, waits for them, and re-layouts, fused_device(): queries.reshape(HELD, STEPS, KVL, GROUP, HD).transpose(0, 2, 1, 3, 4)  1.54 us
    reshape x1, local copies, waits for them, and re-layouts, fused_device(): return out.reshape(32, STEPS, 512)  1.5 us

profile of v1, /device:TPU:0, one launch (start us, length us, event | category | flops | bytes accessed | tf_op | source)
XLA Modules:
  0.0 55.8 jit_solution(16806157584620848657)
XLA Ops:
  0.0 0.7 %reshape.33 = bf16[4,2,4,2,128]{4,3,2,1,0:T(2,128)(2,1)S(1)} reshape(bf16[4,2,4,256]{3,2,1,0:T(4,128)(2,1)} %param.10) | data formatting | bytes 32768 | tf_op jit(solution)/shard_map/reshape | solution.py:576
  0.8 0.9 %reshape.31 = bf16[4,2,4,8,128]{4,3,2,1,0:T(8,128)(2,1)S(1)} reshape(bf16[4,2,4096]{2,1,0:T(2,128)(2,1)} %param.9) | data formatting | bytes 131072 | tf_op jit(solution)/shard_map/reshape | solution.py:574
  1.7 0.6 %copy.10 = bf16[4,2,4,8,128]{4,3,1,2,0:T(8,128)(2,1)} copy(bf16[4,2,4,8,128]{4,3,2,1,0:T(8,128)(2,1)S(1)} %reshape.31) | data formatting | bytes 131072 | tf_op jit(solution)/shard_map/reshape | solution.py:574
  2.3 0.7 %pad.4.new_ref = bf16[4,8,16,128]{3,2,1,0:T(8,128)(2,1)} pad(bf16[4,8,2,128]{3,2,1,0:T(2,128)(2,1)S(1)} %bitcast.17, bf16[]{:T(256)} %constant.2.clone.1), padding=0_0x0_0x0_14x0_0 | pad | bytes 147458 | tf_op jit(solution)/shard_map/jit(_pad)/pad | solution.py:577
  3.0 51.4 %shard_map.91 = bf16[64,512]{1,0:T(8,128)(2,1)} custom-call(s32[4]{0:T(128)} %slen_ref.1, s32[8]{0:T(128)} %plen_ref.1, s32[8]{0:T(128)} %pslot_ref.1, s32[64]{0:T(128)} %bitcast.21, bf16[4,64,128]{2,1,0:T(8,128)(2,1)} %bitcast.18, bf16[4,8,16,128]{3,2,1,0:T(8,128)(2,1)} %pad.4.new_ref, bf16[4,4096,128]{2,1,0:T(8,128)(2,1)} %bitcast.19, ...), custom_call_target="tpu_custom_call" | custom-call | flops 4000000000 | bytes 12000000 | tf_op jit(solution)/shard_map/pallas_call | solution.py:619
  54.3 1.5 %reshape.39 = bf16[32,2,512]{2,1,0:T(2,128)(2,1)} reshape(bf16[64,512]{1,0:T(8,128)(2,1)} %shard_map.91) | data formatting | bytes 131072 | tf_op jit(solution)/shard_map/reshape | solution.py:644
  (1 shorter events, 0.0 us)

commit v2 on v1

--- a/solution.py
+++ b/solution.py
@@ -184,8 +184,10 @@
 KVL = 4
 ROWS = STEPS * GROUP
 SPAN = KVL * ROWS
-LOCAL = SUF + 128
-SCALE = HD ** (-0.5)
+SUF_ROWS = SUF * 2 * KVL
+LOCAL = SUF_ROWS + 128
+FAR = 1 << 20
+SCALE2 = HD ** (-0.5) * math.log2(math.e)
 NT = (((1,), (1,)), ((), ()))
 
 
@@ -205,7 +207,7 @@
     w,
     split_p,
     turn_p,
-    lkv,
+    place,
     pkv,
     qslot,
     qrecv,
@@ -262,7 +264,9 @@
 
     local_copies = [pltpu.make_async_copy(pre_hbm, pre, loc_sem.at[0])]
     local_copies += [
-        pltpu.make_async_copy(suf_hbm.at[s], suf.at[s], loc_sem.at[1 + s]) for s in range(HELD)
+        pltpu.make_async_copy(
+            suf_hbm.at[s], suf.at[s, pl.ds(0, SUF_ROWS)], loc_sem.at[1 + s]
+        ) for s in range(HELD)
     ]
     local_copies.append(pltpu.make_async_copy(w_hbm, w, loc_sem.at[1 + HELD]))
     for copy in local_copies:
@@ -335,57 +339,42 @@
 
     forward(0)
 
-    def split_heads(src, dst):
-        def step(i, carry):
-            first = pl.multiple_of(i * 512, 512)
-            rows = jnp.concatenate(
-                [src[pl.ds(first, 256), :], src[pl.ds(first + 256, 256), :]], axis=1
-            )
-            parted = jnp.dot(split_p[...], rows, preferred_element_type=f32).astype(bf16)
-            to = pl.multiple_of(i * 64, 64)
-            for k in range(8):
-                dst[k, pl.ds(to, 32), :] = parted[k * 32 : (k + 1) * 32, :HD]
-                dst[k, pl.ds(to + 32, 32), :] = parted[k * 32 : (k + 1) * 32, HD:]
-            return carry
-
-        lax.fori_loop(0, 8, step, 0)
-
     local_copies[0].wait()
-    split_heads(pre, pkv)
-
-    lkv[:, SUF:, :] = jnp.zeros((8, LOCAL - SUF, HD), bf16)
-    col = lax.broadcasted_iota(jnp.int32, (ROWS, LOCAL), 1)
-    step_of = lax.broadcasted_iota(jnp.int32, (ROWS, LOCAL), 0) // GROUP
+    for i in range(8):
+        rows = jnp.concatenate(
+            [pre[i * 512 : i * 512 + 256, :], pre[i * 512 + 256 : (i + 1) * 512, :]], axis=1
+        )
+        parted = jnp.dot(split_p[...], rows, preferred_element_type=f32).astype(bf16)
+        for k in range(8):
+            pkv[k, i * 64 : i * 64 + 32, :] = parted[k * 32 : (k + 1) * 32, :HD]
+            pkv[k, i * 64 + 32 : (i + 1) * 64, :] = parted[k * 32 : (k + 1) * 32, HD:]
+
+    col = lax.broadcasted_iota(jnp.int32, (SPAN, LOCAL), 1)
+    row = lax.broadcasted_iota(jnp.int32, (SPAN, LOCAL), 0)
+    spot = col >> 3
+    fresh = jnp.where(spot - SUF <= ((row >> 3) & 1), -1, FAR)
+    place[...] = jnp.where((col & 7) == (row >> 4), jnp.where(spot < SUF, spot, fresh), FAR)
 
     def local_part(s):
         local_copies[1 + s].wait()
-        split_heads(suf.at[s], lkv)
-        lkv[:, SUF : SUF + 16, :] = new_ref[s]
-        limit = jnp.where(col < SUF, slen_ref[s], SUF + 1 + step_of)
-        ok = col < limit
-        for g in range(KVL):
-            query = q_ref[s, g * ROWS : (g + 1) * ROWS, :]
-            scores = lax.dot_general(query, lkv[g], NT, preferred_element_type=f32) * SCALE
-            masked = jnp.where(ok, scores, -1e30)
-            top = jnp.max(masked, axis=1, keepdims=True)
-            weights = jnp.where(ok, jnp.exp(masked - top), 0.0)
-            total = jnp.sum(weights, axis=1, keepdims=True)
-            result = jnp.dot(weights.astype(bf16), lkv[KVL + g], preferred_element_type=f32)
-            here = slice(g * ROWS, (g + 1) * ROWS)
-            lo[s, here, :] = result
-            lm[s, here, :] = jnp.broadcast_to(top, (ROWS, HD))
-            ll[s, here, :] = jnp.broadcast_to(total, (ROWS, HD))
+        suf[s, SUF_ROWS : SUF_ROWS + 16, :] = new_ref[s]
+        suf[s, SUF_ROWS + 16 :, :] = jnp.zeros((LOCAL - SUF_ROWS - 16, HD), bf16)
+        scores = lax.dot_general(q_ref[s], suf[s], NT, preferred_element_type=f32)
+        masked = jnp.where(place[...] < slen_ref[s], scores * SCALE2, -1e30)
+        top = jnp.max(masked, axis=1, keepdims=True)
+        weights = jnp.exp2(masked - top)
+        total = jnp.sum(weights, axis=1, keepdims=True)
+        moved = pltpu.roll(weights, KVL, 1).astype(bf16)
+        lo[s] = jnp.dot(moved, suf[s], preferred_element_type=f32)
+        lm[s] = jnp.broadcast_to(top, (SPAN, HD))
+        ll[s] = jnp.broadcast_to(total, (SPAN, HD))
 
     local_part(0)
     forward(1)
     forward(7)
     local_part(1)
-    forward(2)
-    forward(6)
-    local_part(2)
-    for d in (3, 5, 4):
+    for d in (2, 6, 3, 5, 4):
         forward(d)
-    local_part(3)
 
     usable = lax.broadcasted_iota(jnp.int32, (256, PSH), 1) < prompt_rows - core * PSH
 
@@ -393,10 +382,10 @@
         for g in range(KVL):
             query = qrecv[which, :, :, :].reshape(CHIPS, MOST, KVL, ROWS, HD)[:, :, g]
             query = query.reshape(256, HD)
-            scores = lax.dot_general(query, pkv[g], NT, preferred_element_type=f32) * SCALE
-            masked = jnp.where(usable, scores, -1e30)
+            scores = lax.dot_general(query, pkv[g], NT, preferred_element_type=f32)
+            masked = jnp.where(usable, scores * SCALE2, -1e30)
             top = jnp.max(masked, axis=1, keepdims=True)
-            weights = jnp.where(usable, jnp.exp(masked - top), 0.0)
+            weights = jnp.exp2(masked - top)
             total = jnp.sum(weights, axis=1, keepdims=True)
             result = jnp.dot(weights.astype(bf16), pkv[KVL + g], preferred_element_type=f32)
             shape = (CHIPS, MOST, ROWS, HD)
@@ -443,7 +432,7 @@
         m2 = jnp.broadcast_to(other[0:1], (HD, HD)).T
         l2 = jnp.broadcast_to(other[1:2], (HD, HD)).T
         top = jnp.maximum(m1, m2)
-        w1, w2 = jnp.exp(m1 - top), jnp.exp(m2 - top)
+        w1, w2 = jnp.exp2(m1 - top), jnp.exp2(m2 - top)
         total = w1 * l1 + w2 * l2
         mixed = w1 * half_o[c].reshape(128, HD) + w2 * so_recv[c].astype(f32)
         return (mixed / total).astype(bf16), stat_rows(top, total)
@@ -466,6 +455,8 @@
             copy.start()
             results.append(copy)
     co_recv[chip], cs_recv[chip] = merge(chip)
+    local_part(2)
+    local_part(3)
     for copy in results:
         copy.wait_recv()
 
@@ -480,20 +471,22 @@
         pt = jnp.where(first, totals[:SPAN], totals[SPAN:])
         po = jnp.where(first, block[:SPAN], block[SPAN:])
         overall = jnp.maximum(pm, lm[s])
-        wp = pt * jnp.exp(pm - overall)
-        wl = jnp.exp(lm[s] - overall)
+        wp = pt * jnp.exp2(pm - overall)
+        wl = jnp.exp2(lm[s] - overall)
         parts.append(((wp * po + wl * lo[s]) / (wp + wl * ll[s])).astype(bf16))
     attn = jnp.concatenate(parts, axis=0)
-    ag[wide] = jnp.dot(turn_p[...], attn, preferred_element_type=f32).astype(bf16)
+    turned = jnp.dot(turn_p[...], attn, preferred_element_type=f32).astype(bf16)
+    ag[0, wide] = turned[:128]
+    ag[1, wide] = turned[128:]
 
     sends = []
 
-    def push(index, ss, rs, device):
+    def push(index, ss, rs, i, device):
         copy = pltpu.make_async_remote_copy(
             src_ref=ag.at[index],
             dst_ref=ag.at[index],
-            send_sem=ss,
-            recv_sem=rs,
+            send_sem=ss.at[i],
+            recv_sem=rs.at[i],
             device_id=device,
             device_id_type=MESH,
         )
@@ -502,42 +495,56 @@
         return copy
 
     x_peer = at_chip(zc * 2 + 1 - xc)
-    z_in = {}
-    for d in (2, 1, 3):
-        z_in[d] = push(wide, z_ss.at[d], z_rs.at[d], at_chip(((zc + d) % 4) * 2 + xc))
-    x_in = {0: push(wide, ax_ss.at[0], ax_rs.at[0], x_peer)}
-    c_in = [push(wide, ac_ss.at[0], ac_rs.at[0], sibling)]
-
-    def pass_x(d):
-        x_in[d].wait_recv()
+    z_in, x_in, c_in = {}, {}, ([], [])
+    for h in range(2):
+        x_in[h, 0] = push((h, wide), ax_ss, ax_rs, 4 * h, x_peer)
+        for d in (2, 1, 3):
+            device = at_chip(((zc + d) % 4) * 2 + xc)
+            z_in[h, d] = push((h, wide), z_ss, z_rs, 4 * h + d, device)
+        c_in[h].append(push((h, wide), ac_ss, ac_rs, 8 * h, sibling))
+
+    def pass_x(h, d):
+        x_in[h, d].wait_recv()
         index = (((zc + 4 - d) % 4) * 2 + 1 - xc) * 2 + core
-        c_in.append(push(index, ac_ss.at[4 + d], ac_rs.at[4 + d], sibling))
-
-    def pass_z(d):
-        z_in[d].wait_recv()
+        c_in[h].append(push((h, index), ac_ss, ac_rs, 8 * h + 4 + d, sibling))
+
+    def pass_z(h, d):
+        z_in[h, d].wait_recv()
         index = (((zc + 4 - d) % 4) * 2 + xc) * 2 + core
-        x_in[d] = push(index, ax_ss.at[d], ax_rs.at[d], x_peer)
-        c_in.append(push(index, ac_ss.at[d], ac_rs.at[d], sibling))
+        x_in[h, d] = push((h, index), ax_ss, ax_rs, 4 * h + d, x_peer)
+        c_in[h].append(push((h, index), ac_ss, ac_rs, 8 * h + d, sibling))
+
+    def gather_rows(h):
+        for copy in c_in[h]:
+            copy.wait_recv()
+        for k in range(8):
+            block = ag[h, :, k * 16 : (k + 1) * 16, :].astype(f32)
+            to = h * 2048 + k * 256
+            lhs[:, to : to + 128] = block[:, :8].reshape(128, HD).astype(bf16)
+            lhs[:, to + 128 : to + 256] = block[:, 8:].reshape(128, HD).astype(bf16)
 
     for d in (1, 3, 2):
-        pass_z(d)
+        pass_z(0, d)
     for d in (0, 1, 3, 2):
-        pass_x(d)
+        pass_x(0, d)
+    for d in (1, 3, 2):
+        pass_z(1, d)
     local_copies[1 + HELD].wait()
-    for copy in c_in:
-        copy.wait_recv()
-
-    for k in range(16):
-        block = ag[:, k * 16 : (k + 1) * 16, :].astype(f32)
-        lhs[:, k * 256 : k * 256 + 128] = block[:, :8].reshape(128, HD).astype(bf16)
-        lhs[:, k * 256 + 128 : (k + 1) * 256] = block[:, 8:].reshape(128, HD).astype(bf16)
+    gather_rows(0)
+    for n in range(2):
+        terms[n] = jnp.dot(
+            lhs[:, :2048], w[:2048, n * 256 : (n + 1) * 256], preferred_element_type=f32
+        )
+    for d in (0, 1, 3, 2):
+        pass_x(1, d)
+    gather_rows(1)
 
     theirs = pl.multiple_of((1 - y) * 64, 64)
     mine = pl.multiple_of(y * 64, 64)
     y_copies = []
     for n in range(2):
-        terms[n] = jnp.dot(
-            lhs[...], w[:, n * 256 : (n + 1) * 256], preferred_element_type=f32
+        terms[n] += jnp.dot(
+            lhs[:, 2048:], w[2048:, n * 256 : (n + 1) * 256], preferred_element_type=f32
         )
         y_send[n] = terms[n, pl.ds(theirs, 64), :].astype(bf16)
         copy = pltpu.make_async_remote_copy(
@@ -573,10 +580,8 @@
     f32, bf16 = jnp.float32, jnp.bfloat16
     q_rows = queries.reshape(HELD, STEPS, KVL, GROUP, HD).transpose(0, 2, 1, 3, 4)
     q_rows = q_rows.reshape(HELD, SPAN, HD)
-    new_rows = new_kv.reshape(HELD, STEPS, KVL, 2, HD).transpose(0, 3, 2, 1, 4)
-    new_rows = jnp.pad(
-        new_rows.reshape(HELD, 2 * KVL, STEPS, HD), ((0, 0), (0, 0), (0, 16 - STEPS), (0, 0))
-    )
+    new_rows = new_kv.reshape(HELD, STEPS, KVL, 2, HD).transpose(0, 1, 3, 2, 4)
+    new_rows = new_rows.reshape(HELD, STEPS * 8, HD)
     suf = suffix_cache.reshape(HELD, SUF, KVL, 2, HD).transpose(0, 1, 3, 2, 4)
     suf = suf.reshape(HELD, SUF * 8, HD)
     pre = prefix_cache.reshape(PSH, KVL, 2, HD).transpose(0, 2, 1, 3).reshape(PSH * 8, HD)
@@ -584,12 +589,12 @@
     dma = pltpu.SemaphoreType.DMA
     half = (CHIPS, MOST, KVL, ROWS, HD)
     scratch = [
-        vm((HELD, SUF * 8, HD), bf16),
+        vm((HELD, LOCAL, HD), bf16),
         vm((PSH * 8, HD), bf16),
         vm((KVL * 1024, 512), bf16),
         vm((256, 256), bf16),
         vm((256, 256), bf16),
-        vm((8, LOCAL, HD), bf16),
+        vm((SPAN, LOCAL), jnp.int32),
         vm((8, PSH, HD), bf16),
         vm((CHIPS, 128, HD), bf16),
         vm((2, CHIPS, 128, HD), bf16),
@@ -607,14 +612,14 @@
         vm((CHIPS, 8, HD), f32),
         vm((CHIPS, 128, HD), bf16),
         vm((CHIPS, 8, HD), f32),
-        vm((16, 256, HD), bf16),
+        vm((2, 16, 128, HD), bf16),
         vm((128, 4096), bf16),
         vm((2, 128, 256), f32),
         vm((2, 64, 256), bf16),
         vm((2, 64, 256), bf16),
         dma((2 + HELD,)),
     ]
-    for count in (8, 8, 2, 8, 8, 4, 4, 8, 2):
+    for count in (8, 8, 2, 8, 8, 8, 8, 16, 2):
         scratch += [dma((count,)), dma((count,))]
     out = pl.pallas_call(
         fused_kernel,

time: 56.1 us -> 48.9 us (0.87)
  Pallas kernels: 51.4 us -> 45.6 us
  local copies, waits for them, and re-layouts: 4.44 us -> 3.04 us
    pallas_call x1, Pallas kernels: 51.4 us -> 45.6 us  [fused_device(): pl.pallas_call(fused_kernel, out_shape=jax.ShapeDtypeStruct((64, 512), bf...]
    reshape x2 -> x0, local copies, waits for them, and re-layouts: 0.75 us -> none  [fused_device(): new_rows = new_kv.reshape(HELD, STEPS, KVL, 2, HD).transpose(0, 3, 2, 1, 4)]
    pad x1 -> x0, local copies, waits for them, and re-layouts: 0.66 us -> none  [fused_device(): jnp.pad(new_rows.reshape(HELD, 2 * KVL, STEPS, HD), ((0, 0), (0, 0), (0,...]
where the time goes in v2:
time: 48.9 us; the launch traced here: 48.7 us
  Pallas kernels  45.6 us (93%)
  local copies, waits for them, and re-layouts  3.04 us (6%)
    pallas_call x1, Pallas kernels, fused_device(): pl.pallas_call(fused_kernel, out_shape=jax.ShapeDtypeStruct((64, 512), bf...  45.6 us
    reshape x2, local copies, waits for them, and re-layouts, fused_device(): queries.reshape(HELD, STEPS, KVL, GROUP, HD).transpose(0, 2, 1, 3, 4)  1.54 us
    reshape x1, local copies, waits for them, and re-layouts, fused_device(): return out.reshape(32, STEPS, 512)  1.5 us

profile of v2, /device:TPU:0, one launch (start us, length us, event | category | flops | bytes accessed | tf_op | source)
XLA Modules:
  0.0 48.7 jit_solution(5528093225703818753)
XLA Ops:
  0.0 0.9 %reshape.31 = bf16[4,2,4,8,128]{4,3,2,1,0:T(8,128)(2,1)S(1)} reshape(bf16[4,2,4096]{2,1,0:T(2,128)(2,1)} %param.9) | data formatting | bytes 131072 | tf_op jit(solution)/shard_map/reshape | solution.py:581
  0.9 0.6 %copy.10 = bf16[4,2,4,8,128]{4,3,1,2,0:T(8,128)(2,1)} copy(bf16[4,2,4,8,128]{4,3,2,1,0:T(8,128)(2,1)S(1)} %reshape.31) | data formatting | bytes 131072 | tf_op jit(solution)/shard_map/reshape | solution.py:581
  1.5 45.6 %shard_map.91 = bf16[64,512]{1,0:T(8,128)(2,1)} custom-call(s32[4]{0:T(128)} %slen_ref.1, s32[8]{0:T(128)} %plen_ref.1, s32[8]{0:T(128)} %pslot_ref.1, s32[64]{0:T(128)} %bitcast.23, bf16[4,64,128]{2,1,0:T(8,128)(2,1)} %bitcast.19, bf16[4,16,128]{2,1,0:T(8,128)(2,1)} %bitcast.22, bf16[4,4096,128]{2,1,0:T(8,128)(2,1)} %bitcast.20, ...), custom_call_target="tpu_custom_call" | custom-call | flops 4000000000 | bytes 12000000 | tf_op jit(solution)/shard_map/pallas_call | solution.py:624
  47.2 1.5 %reshape.39 = bf16[32,2,512]{2,1,0:T(2,128)(2,1)} reshape(bf16[64,512]{1,0:T(8,128)(2,1)} %shard_map.91) | data formatting | bytes 131072 | tf_op jit(solution)/shard_map/reshape | solution.py:649

commit v3 on v2

--- a/solution.py
+++ b/solution.py
@@ -184,6 +184,8 @@
 KVL = 4
 ROWS = STEPS * GROUP
 SPAN = KVL * ROWS
+PART = SPAN // 2
+PAIR = MOST * PART
 SUF_ROWS = SUF * 2 * KVL
 LOCAL = SUF_ROWS + 128
 FAR = 1 << 20
@@ -207,6 +209,7 @@
     w,
     split_p,
     turn_p,
+    out_p,
     place,
     pkv,
     qslot,
@@ -223,8 +226,10 @@
     st_recv,
     co_send,
     cs_send,
-    co_recv,
-    cs_recv,
+    co_first,
+    cs_first,
+    co_second,
+    cs_second,
     ag,
     lhs,
     terms,
@@ -293,7 +298,9 @@
             pick = jnp.int32(0)
             for s in range(1, HELD):
                 pick = pick + jnp.where((groups[s] == c) & (ranks[s] == m), s, 0)
-            qslot[c, m * SPAN : (m + 1) * SPAN, :] = q_ref[pick]
+            chosen = q_ref[pick]
+            for h in range(2):
+                qslot[h, c, m * PART : (m + 1) * PART, :] = chosen[h * PART : (h + 1) * PART]
     prompt_rows = jnp.int32(0)
     for p in range(NPROMPT):
         prompt_rows = prompt_rows + jnp.where(pslot_ref[p] == chip, plen_ref[p], 0)
@@ -301,43 +308,46 @@
     out_row = lax.broadcasted_iota(jnp.int32, (256, 256), 0)
     in_row = lax.broadcasted_iota(jnp.int32, (256, 256), 1)
     split_p[...] = jnp.where(in_row == (out_row & 31) * 8 + (out_row >> 5), 1.0, 0.0).astype(bf16)
-    source = (
-        ((out_row >> 1) & 3) * 64 + (out_row >> 6) * 16 + (out_row & 1) * 8 + ((out_row >> 3) & 7)
-    )
-    turn_p[...] = jnp.where(in_row == source, 1.0, 0.0).astype(bf16)
+    gathered = ((out_row >> 1) & 3) * 64 + (out_row >> 3) * 2 + (out_row & 1)
+    out_p[...] = jnp.where(in_row == gathered, 1.0, 0.0).astype(bf16)
+    to_row, from_row = out_row[:128, :128], in_row[:128, :128]
+    source = ((to_row >> 1) & 3) * PART + (to_row >> 3) * 2 + (to_row & 1)
+    turn_p[...] = jnp.where(from_row == source, 1.0, 0.0).astype(bf16)
 
     pl.semaphore_wait(barrier, CHIPS + 1)
 
     q_copies = {}
-    for d in (4, 3, 5, 2, 6, 1, 7):
-        dst = (chip + d) % CHIPS
-        q_copies[d] = pltpu.make_async_remote_copy(
-            src_ref=qslot.at[dst],
-            dst_ref=qrecv.at[core, chip],
-            send_sem=q_ss.at[d],
-            recv_sem=q_rs.at[d],
-            device_id=at_chip(dst),
-            device_id_type=MESH,
-        )
-        q_copies[d].start()
-    qrecv[core, chip] = qslot[chip]
+    for h in range(2):
+        for d in (4, 3, 5, 2, 6, 1, 7):
+            dst = (chip + d) % CHIPS
+            q_copies[h, d] = pltpu.make_async_remote_copy(
+                src_ref=qslot.at[h, dst],
+                dst_ref=qrecv.at[h, core, chip],
+                send_sem=q_ss.at[8 * h + d],
+                recv_sem=q_rs.at[8 * h + d],
+                device_id=at_chip(dst),
+                device_id_type=MESH,
+            )
+            q_copies[h, d].start()
+        qrecv[h, core, chip] = qslot[h, chip]
     forwards = {}
 
-    def forward(d):
+    def forward(h, d):
         src = (chip + CHIPS - d) % CHIPS
         if d:
-            q_copies[d].wait_recv()
-        forwards[d] = pltpu.make_async_remote_copy(
-            src_ref=qrecv.at[core, src],
-            dst_ref=qrecv.at[core, src],
-            send_sem=qf_ss.at[d],
-            recv_sem=qf_rs.at[d],
+            q_copies[h, d].wait_recv()
+        forwards[h, d] = pltpu.make_async_remote_copy(
+            src_ref=qrecv.at[h, core, src],
+            dst_ref=qrecv.at[h, core, src],
+            send_sem=qf_ss.at[8 * h + d],
+            recv_sem=qf_rs.at[8 * h + d],
             device_id=sibling,
             device_id_type=MESH,
         )
-        forwards[d].start()
-
-    forward(0)
+        forwards[h, d].start()
+
+    forward(0, 0)
+    forward(1, 0)
 
     local_copies[0].wait()
     for i in range(8):
@@ -352,7 +362,7 @@
     col = lax.broadcasted_iota(jnp.int32, (SPAN, LOCAL), 1)
     row = lax.broadcasted_iota(jnp.int32, (SPAN, LOCAL), 0)
     spot = col >> 3
-    fresh = jnp.where(spot - SUF <= ((row >> 3) & 1), -1, FAR)
+    fresh = jnp.where(spot - SUF <= (row & 1), -1, FAR)
     place[...] = jnp.where((col & 7) == (row >> 4), jnp.where(spot < SUF, spot, fresh), FAR)
 
     def local_part(s):
@@ -370,18 +380,17 @@
         ll[s] = jnp.broadcast_to(total, (SPAN, HD))
 
     local_part(0)
-    forward(1)
-    forward(7)
+    for d in (1, 7, 2, 6, 3, 5, 4):
+        forward(0, d)
     local_part(1)
-    for d in (2, 6, 3, 5, 4):
-        forward(d)
 
     usable = lax.broadcasted_iota(jnp.int32, (256, PSH), 1) < prompt_rows - core * PSH
 
-    def prefix_half(which):
-        for g in range(KVL):
-            query = qrecv[which, :, :, :].reshape(CHIPS, MOST, KVL, ROWS, HD)[:, :, g]
-            query = query.reshape(256, HD)
+    def prefix_half(h, which):
+        queries = qrecv[h, which].reshape(CHIPS, MOST, 2, ROWS, HD)
+        for e in range(2):
+            g = 2 * h + e
+            query = queries[:, :, e].reshape(256, HD)
             scores = lax.dot_general(query, pkv[g], NT, preferred_element_type=f32)
             masked = jnp.where(usable, scores * SCALE2, -1e30)
             top = jnp.max(masked, axis=1, keepdims=True)
@@ -389,95 +398,100 @@
             total = jnp.sum(weights, axis=1, keepdims=True)
             result = jnp.dot(weights.astype(bf16), pkv[KVL + g], preferred_element_type=f32)
             shape = (CHIPS, MOST, ROWS, HD)
-            half_o[:, :, g] = result.reshape(shape)
-            half_m[:, :, g] = jnp.broadcast_to(top, (256, HD)).reshape(shape)
-            half_l[:, :, g] = jnp.broadcast_to(total, (256, HD)).reshape(shape)
-
-    sub = lax.broadcasted_iota(jnp.int32, (8, HD), 0)
+            half_o[:, :, e] = result.reshape(shape)
+            half_m[:, :, e] = jnp.broadcast_to(top, (256, HD)).reshape(shape)
+            half_l[:, :, e] = jnp.broadcast_to(total, (256, HD)).reshape(shape)
 
     def stat_rows(top, total):
-        return jnp.where(sub == 0, top.T[:8], total.T[:8])
-
-    for d in (0, 1, 2, 3, 4, 5, 6, 7):
-        forwards[d].wait_recv()
-    prefix_half(1 - core)
-
-    def pack_half(c, carry):
-        so_send[c] = half_o[c].reshape(128, HD).astype(bf16)
-        st_send[c] = stat_rows(half_m[c].reshape(128, HD), half_l[c].reshape(128, HD))
-        return carry
-
-    lax.fori_loop(0, CHIPS, pack_half, 0)
+        return jnp.concatenate([top, total], axis=0).T[:8]
+
+    def flat(ref, c):
+        return ref[c].reshape(PAIR, HD)
+
+    co_recv, cs_recv = (co_first, co_second), (cs_first, cs_second)
     swaps = []
-    for i, (src, dst) in enumerate(((so_send, so_recv), (st_send, st_recv))):
-        copy = pltpu.make_async_remote_copy(
-            src_ref=src,
-            dst_ref=dst,
-            send_sem=x_ss.at[i],
-            recv_sem=x_rs.at[i],
-            device_id=sibling,
-            device_id_type=MESH,
-        )
-        copy.start()
-        swaps.append(copy)
-    prefix_half(core)
-    for copy in swaps:
-        copy.wait_recv()
-
-    results = []
-
-    def merge(c):
-        m1, l1 = half_m[c].reshape(128, HD), half_l[c].reshape(128, HD)
-        other = st_recv[c]
-        m2 = jnp.broadcast_to(other[0:1], (HD, HD)).T
-        l2 = jnp.broadcast_to(other[1:2], (HD, HD)).T
+    results = {}
+
+    def merge(h, c):
+        m1, l1 = flat(half_m, c), flat(half_l, c)
+        other = jnp.broadcast_to(st_recv[h, c][0:1], (HD, HD)).T
+        m2, l2 = other[:PAIR], other[PAIR:]
         top = jnp.maximum(m1, m2)
         w1, w2 = jnp.exp2(m1 - top), jnp.exp2(m2 - top)
         total = w1 * l1 + w2 * l2
-        mixed = w1 * half_o[c].reshape(128, HD) + w2 * so_recv[c].astype(f32)
+        mixed = w1 * flat(half_o, c) + w2 * so_recv[h, c].astype(f32)
         return (mixed / total).astype(bf16), stat_rows(top, total)
 
-    for d in (4, 3, 5, 2, 6, 1, 7):
-        dst = (chip + d) % CHIPS
-        co_send[dst], cs_send[dst] = merge(dst)
-        for src, target, ss, rs in (
-            (co_send, co_recv, c_ss, c_rs),
-            (cs_send, cs_recv, s_ss, s_rs),
-        ):
+    def prefix_part(h):
+        for d in range(CHIPS):
+            forwards[h, d].wait_recv()
+        prefix_half(h, 1 - core)
+        for c in range(CHIPS):
+            so_send[h, c] = flat(half_o, c).astype(bf16)
+            st_send[h, c] = stat_rows(flat(half_m, c), flat(half_l, c))
+        mine = []
+        for i, (src, dst) in enumerate(((so_send, so_recv), (st_send, st_recv))):
             copy = pltpu.make_async_remote_copy(
-                src_ref=src.at[dst],
-                dst_ref=target.at[chip],
-                send_sem=ss.at[d],
-                recv_sem=rs.at[d],
-                device_id=at_chip(dst),
+                src_ref=src.at[h],
+                dst_ref=dst.at[h],
+                send_sem=x_ss.at[2 * h + i],
+                recv_sem=x_rs.at[2 * h + i],
+                device_id=sibling,
                 device_id_type=MESH,
             )
             copy.start()
-            results.append(copy)
-    co_recv[chip], cs_recv[chip] = merge(chip)
+            mine.append(copy)
+        swaps.extend(mine)
+        prefix_half(h, core)
+        for copy in mine:
+            copy.wait_recv()
+        for d in (4, 3, 5, 2, 6, 1, 7):
+            dst = (chip + d) % CHIPS
+            co_send[h, dst], cs_send[h, dst] = merge(h, dst)
+            for src, target, ss, rs in (
+                (co_send, co_recv, c_ss, c_rs),
+                (cs_send, cs_recv, s_ss, s_rs),
+            ):
+                copy = pltpu.make_async_remote_copy(
+                    src_ref=src.at[h, dst],
+                    dst_ref=target[h].at[chip],
+                    send_sem=ss.at[8 * h + d],
+                    recv_sem=rs.at[8 * h + d],
+                    device_id=at_chip(dst),
+                    device_id_type=MESH,
+                )
+                copy.start()
+                results.setdefault(h, []).append(copy)
+        co_recv[h][chip], cs_recv[h][chip] = merge(h, chip)
+
+    prefix_part(0)
+    for d in (1, 7, 2, 6, 3, 5, 4):
+        forward(1, d)
     local_part(2)
+    prefix_part(1)
     local_part(3)
-    for copy in results:
-        copy.wait_recv()
-
-    parts = []
-    for s in range(HELD):
-        stats = cs_recv[groups[s]]
-        block = co_recv[groups[s]].astype(f32)
-        first = jnp.broadcast_to(ranks[s] == 0, (SPAN, HD))
-        tops = jnp.broadcast_to(stats[0:1], (HD, HD)).T
-        totals = jnp.broadcast_to(stats[1:2], (HD, HD)).T
-        pm = jnp.where(first, tops[:SPAN], tops[SPAN:])
-        pt = jnp.where(first, totals[:SPAN], totals[SPAN:])
-        po = jnp.where(first, block[:SPAN], block[SPAN:])
-        overall = jnp.maximum(pm, lm[s])
-        wp = pt * jnp.exp2(pm - overall)
-        wl = jnp.exp2(lm[s] - overall)
-        parts.append(((wp * po + wl * lo[s]) / (wp + wl * ll[s])).astype(bf16))
-    attn = jnp.concatenate(parts, axis=0)
-    turned = jnp.dot(turn_p[...], attn, preferred_element_type=f32).astype(bf16)
-    ag[0, wide] = turned[:128]
-    ag[1, wide] = turned[128:]
+
+    def attention(h):
+        for copy in results[h]:
+            copy.wait_recv()
+        here = slice(h * PART, (h + 1) * PART)
+        parts = []
+        for s in range(HELD):
+            stats = jnp.broadcast_to(cs_recv[h][groups[s]][0:1], (HD, HD)).T
+            block = co_recv[h][groups[s]].astype(f32)
+            first = jnp.broadcast_to(ranks[s] == 0, (PART, HD))
+            pm = jnp.where(first, stats[:PART], stats[PART:PAIR])
+            pt = jnp.where(first, stats[PAIR : PAIR + PART], stats[PAIR + PART :])
+            po = jnp.where(first, block[:PART], block[PART:])
+            own = lm[s, here, :]
+            overall = jnp.maximum(pm, own)
+            wp = pt * jnp.exp2(pm - overall)
+            wl = jnp.exp2(own - overall)
+            mixed = wp * po + wl * lo[s, here, :]
+            parts.append((mixed / (wp + wl * ll[s, here, :])).astype(bf16))
+        attn = jnp.concatenate(parts, axis=0)
+        turned = jnp.dot(turn_p[...], attn, preferred_element_type=f32)
+        ag[h, wide] = turned.astype(bf16)
 
     sends = []
 
@@ -497,6 +511,7 @@
     x_peer = at_chip(zc * 2 + 1 - xc)
     z_in, x_in, c_in = {}, {}, ([], [])
     for h in range(2):
+        attention(h)
         x_in[h, 0] = push((h, wide), ax_ss, ax_rs, 4 * h, x_peer)
         for d in (2, 1, 3):
             device = at_chip(((zc + d) % 4) * 2 + xc)
@@ -557,12 +572,16 @@
         )
         copy.start()
         y_copies.append(copy)
+    finals = []
     for n in range(2):
         y_copies[n].wait_recv()
         total = terms[n, pl.ds(mine, 64), :] + y_recv[n].astype(f32)
-        o_ref[:, n * 256 : (n + 1) * 256] = total.astype(bf16)
-
-    for copy in [*q_copies.values(), *forwards.values(), *swaps, *results, *sends, *y_copies]:
+        finals += [total[:, :HD].astype(bf16), total[:, HD:].astype(bf16)]
+    o_ref[...] = jnp.dot(
+        out_p[...], jnp.concatenate(finals, axis=0), preferred_element_type=f32
+    ).astype(bf16)
+
+    for copy in [*sends, *y_copies, *q_copies.values(), *forwards.values(), *swaps, *results[0], *results[1]]:
         copy.wait_send()
 
 
@@ -578,7 +597,7 @@
     out_weight,
 ):
     f32, bf16 = jnp.float32, jnp.bfloat16
-    q_rows = queries.reshape(HELD, STEPS, KVL, GROUP, HD).transpose(0, 2, 1, 3, 4)
+    q_rows = queries.reshape(HELD, STEPS, KVL * GROUP, HD).transpose(0, 2, 1, 3)
     q_rows = q_rows.reshape(HELD, SPAN, HD)
     new_rows = new_kv.reshape(HELD, STEPS, KVL, 2, HD).transpose(0, 1, 3, 2, 4)
     new_rows = new_rows.reshape(HELD, STEPS * 8, HD)
@@ -587,30 +606,34 @@
     pre = prefix_cache.reshape(PSH, KVL, 2, HD).transpose(0, 2, 1, 3).reshape(PSH * 8, HD)
     vm, sm, hbm = pltpu.VMEM, pltpu.SMEM, pl.ANY
     dma = pltpu.SemaphoreType.DMA
-    half = (CHIPS, MOST, KVL, ROWS, HD)
+    half = (CHIPS, MOST, 2, ROWS, HD)
+    block, stat = vm((2, CHIPS, PAIR, HD), bf16), vm((2, CHIPS, 8, HD), f32)
     scratch = [
         vm((HELD, LOCAL, HD), bf16),
         vm((PSH * 8, HD), bf16),
         vm((KVL * 1024, 512), bf16),
         vm((256, 256), bf16),
+        vm((128, 128), bf16),
         vm((256, 256), bf16),
         vm((SPAN, LOCAL), jnp.int32),
         vm((8, PSH, HD), bf16),
-        vm((CHIPS, 128, HD), bf16),
-        vm((2, CHIPS, 128, HD), bf16),
+        block,
+        vm((2, 2, CHIPS, PAIR, HD), bf16),
         vm((HELD, SPAN, HD), f32),
         vm((HELD, SPAN, HD), f32),
         vm((HELD, SPAN, HD), f32),
         vm(half, f32),
         vm(half, f32),
         vm(half, f32),
-        vm((CHIPS, 128, HD), bf16),
+        block,
+        stat,
+        block,
+        stat,
+        block,
+        stat,
+        vm((CHIPS, PAIR, HD), bf16),
         vm((CHIPS, 8, HD), f32),
-        vm((CHIPS, 128, HD), bf16),
-        vm((CHIPS, 8, HD), f32),
-        vm((CHIPS, 128, HD), bf16),
-        vm((CHIPS, 8, HD), f32),
-        vm((CHIPS, 128, HD), bf16),
+        vm((CHIPS, PAIR, HD), bf16),
         vm((CHIPS, 8, HD), f32),
         vm((2, 16, 128, HD), bf16),
         vm((128, 4096), bf16),
@@ -619,11 +642,11 @@
         vm((2, 64, 256), bf16),
         dma((2 + HELD,)),
     ]
-    for count in (8, 8, 2, 8, 8, 8, 8, 16, 2):
+    for count in (16, 16, 4, 16, 16, 8, 8, 16, 2):
         scratch += [dma((count,)), dma((count,))]
     out = pl.pallas_call(
         fused_kernel,
-        out_shape=jax.ShapeDtypeStruct((64, 512), bf16),
+        out_shape=jax.ShapeDtypeStruct((256, HD), bf16),
         in_specs=[pl.BlockSpec(memory_space=sm)] * 4
         + [pl.BlockSpec(memory_space=vm)] * 2
         + [pl.BlockSpec(memory_space=hbm)] * 3,
@@ -646,7 +669,7 @@
         pre,
         out_weight,
     )
-    return out.reshape(32, STEPS, 512)
+    return out.reshape(32, 4, STEPS, HD).transpose(0, 2, 1, 3).reshape(32, STEPS, 512)
 
 
 def solution(mesh):

time: 48.9 us -> 44.2 us (0.904)
  Pallas kernels: 45.6 us -> 42.3 us
  local copies, waits for them, and re-layouts: 3.04 us -> 1.52 us
    pallas_call x1, Pallas kernels: 45.6 us -> 42.3 us  [fused_device(): pl.pallas_call(fused_kernel, out_shape=jax.ShapeDtypeStruct((256, HD), bf...]
    reshape x3 -> x0, local copies, waits for them, and re-layouts: 3.04 us -> none  [the longest x2 1.54 us: fused_device(): queries.reshape(HELD, STEPS, KVL, GROUP, HD).transpose(0, 2, 1, 3, 4)]
    unnamed x0 -> x1, local copies, waits for them, and re-layouts: none -> 1.52 us
where the time goes in v3:
time: 44.2 us; the launch traced here: 43.8 us
  Pallas kernels  42.3 us (96%)
  local copies, waits for them, and re-layouts  1.52 us (3%)
    pallas_call x1, Pallas kernels, fused_device(): pl.pallas_call(fused_kernel, out_shape=jax.ShapeDtypeStruct((256, HD), bf...  42.3 us
    unnamed x1, local copies, waits for them, and re-layouts  1.52 us

profile of v3, /device:TPU:0, one launch (start us, length us, event | category | flops | bytes accessed | tf_op | source)
XLA Modules:
  0.0 43.8 jit_solution(6636209403791158248)
XLA Ops:
  0.0 42.3 %shard_map.91 = bf16[256,128]{1,0:T(8,128)(2,1)} custom-call(s32[4]{0:T(128)} %slen_ref.1, s32[8]{0:T(128)} %plen_ref.1, s32[8]{0:T(128)} %pslot_ref.1, s32[64]{0:T(128)} %bitcast.31, bf16[4,64,128]{2,1,0:T(8,128)(2,1)} %bitcast.29, bf16[4,16,128]{2,1,0:T(8,128)(2,1)} %bitcast.30, bf16[4,4096,128]{2,1,0:T(8,128)(2,1)} %bitcast.27, ...), custom_call_target="tpu_custom_call" | custom-call | flops 4000000000 | bytes 12000000 | tf_op jit(solution)/shard_map/pallas_call | solution.py:647
  42.3 1.5 %copy.16 = bf16[32,2,512]{2,1,0:T(2,128)(2,1)} copy(bf16[32,2,512]{2,1,0:T(2,128)(2,1)} %bitcast.26) | data formatting | bytes 131072

commit v4 on v3

--- a/solution.py
+++ b/solution.py
@@ -187,7 +187,8 @@
 PART = SPAN // 2
 PAIR = MOST * PART
 SUF_ROWS = SUF * 2 * KVL
-LOCAL = SUF_ROWS + 128
+LOCAL = SUF_ROWS + 256
+WING = LOCAL // 2
 FAR = 1 << 20
 SCALE2 = HD ** (-0.5) * math.log2(math.e)
 NT = (((1,), (1,)), ((), ()))
@@ -305,15 +306,6 @@
     for p in range(NPROMPT):
         prompt_rows = prompt_rows + jnp.where(pslot_ref[p] == chip, plen_ref[p], 0)
 
-    out_row = lax.broadcasted_iota(jnp.int32, (256, 256), 0)
-    in_row = lax.broadcasted_iota(jnp.int32, (256, 256), 1)
-    split_p[...] = jnp.where(in_row == (out_row & 31) * 8 + (out_row >> 5), 1.0, 0.0).astype(bf16)
-    gathered = ((out_row >> 1) & 3) * 64 + (out_row >> 3) * 2 + (out_row & 1)
-    out_p[...] = jnp.where(in_row == gathered, 1.0, 0.0).astype(bf16)
-    to_row, from_row = out_row[:128, :128], in_row[:128, :128]
-    source = ((to_row >> 1) & 3) * PART + (to_row >> 3) * 2 + (to_row & 1)
-    turn_p[...] = jnp.where(from_row == source, 1.0, 0.0).astype(bf16)
-
     pl.semaphore_wait(barrier, CHIPS + 1)
 
     q_copies = {}
@@ -349,6 +341,15 @@
     forward(0, 0)
     forward(1, 0)
 
+    out_row = lax.broadcasted_iota(jnp.int32, (256, 256), 0)
+    in_row = lax.broadcasted_iota(jnp.int32, (256, 256), 1)
+    split_p[...] = jnp.where(in_row == (out_row & 31) * 8 + (out_row >> 5), 1.0, 0.0).astype(bf16)
+    gathered = ((out_row >> 1) & 3) * 64 + (out_row >> 3) * 2 + (out_row & 1)
+    out_p[...] = jnp.where(in_row == gathered, 1.0, 0.0).astype(bf16)
+    to_row, from_row = out_row[:128, :128], in_row[:128, :128]
+    source = ((to_row >> 1) & 3) * PART + (to_row >> 3) * 2 + (to_row & 1)
+    turn_p[...] = jnp.where(from_row == source, 1.0, 0.0).astype(bf16)
+
     local_copies[0].wait()
     for i in range(8):
         rows = jnp.concatenate(
@@ -359,25 +360,37 @@
             pkv[k, i * 64 : i * 64 + 32, :] = parted[k * 32 : (k + 1) * 32, :HD]
             pkv[k, i * 64 + 32 : (i + 1) * 64, :] = parted[k * 32 : (k + 1) * 32, HD:]
 
-    col = lax.broadcasted_iota(jnp.int32, (SPAN, LOCAL), 1)
-    row = lax.broadcasted_iota(jnp.int32, (SPAN, LOCAL), 0)
-    spot = col >> 3
+    col = lax.broadcasted_iota(jnp.int32, (2 * SPAN, WING), 1)
+    row = lax.broadcasted_iota(jnp.int32, (2 * SPAN, WING), 0)
+    spot = (col + jnp.where(row < SPAN, 0, WING)) >> 3
     fresh = jnp.where(spot - SUF <= (row & 1), -1, FAR)
-    place[...] = jnp.where((col & 7) == (row >> 4), jnp.where(spot < SUF, spot, fresh), FAR)
+    head = (row >> 4) & (KVL - 1)
+    place[...] = jnp.where((col & 7) == head, jnp.where(spot < SUF, spot, fresh), FAR)
+    blank = jnp.zeros((SPAN, HD), bf16)
 
     def local_part(s):
         local_copies[1 + s].wait()
         suf[s, SUF_ROWS : SUF_ROWS + 16, :] = new_ref[s]
         suf[s, SUF_ROWS + 16 :, :] = jnp.zeros((LOCAL - SUF_ROWS - 16, HD), bf16)
-        scores = lax.dot_general(q_ref[s], suf[s], NT, preferred_element_type=f32)
+        wings = jnp.concatenate([suf[s, :WING, :], suf[s, WING:, :]], axis=1)
+        query = jnp.concatenate(
+            [
+                jnp.concatenate([q_ref[s], blank], axis=1),
+                jnp.concatenate([blank, q_ref[s]], axis=1),
+            ],
+            axis=0,
+        )
+        scores = lax.dot_general(query, wings, NT, preferred_element_type=f32)
         masked = jnp.where(place[...] < slen_ref[s], scores * SCALE2, -1e30)
         top = jnp.max(masked, axis=1, keepdims=True)
-        weights = jnp.exp2(masked - top)
+        top = jnp.maximum(top[:SPAN], top[SPAN:])
+        weights = jnp.exp2(masked - jnp.concatenate([top, top], axis=0))
         total = jnp.sum(weights, axis=1, keepdims=True)
         moved = pltpu.roll(weights, KVL, 1).astype(bf16)
-        lo[s] = jnp.dot(moved, suf[s], preferred_element_type=f32)
+        mixed = jnp.dot(moved, wings, preferred_element_type=f32)
+        lo[s] = mixed[:SPAN, :HD] + mixed[SPAN:, HD:]
         lm[s] = jnp.broadcast_to(top, (SPAN, HD))
-        ll[s] = jnp.broadcast_to(total, (SPAN, HD))
+        ll[s] = jnp.broadcast_to(total[:SPAN] + total[SPAN:], (SPAN, HD))
 
     local_part(0)
     for d in (1, 7, 2, 6, 3, 5, 4):
@@ -467,8 +480,8 @@
     prefix_part(0)
     for d in (1, 7, 2, 6, 3, 5, 4):
         forward(1, d)
+    prefix_part(1)
     local_part(2)
-    prefix_part(1)
     local_part(3)
 
     def attention(h):
@@ -615,7 +628,7 @@
         vm((256, 256), bf16),
         vm((128, 128), bf16),
         vm((256, 256), bf16),
-        vm((SPAN, LOCAL), jnp.int32),
+        vm((2 * SPAN, WING), jnp.int32),
         vm((8, PSH, HD), bf16),
         block,
         vm((2, 2, CHIPS, PAIR, HD), bf16),

time: 44.2 us -> 45.5 us (1.029)
  Pallas kernels: 42.3 us -> 43.2 us
    pallas_call x1, Pallas kernels: 42.3 us -> 43.2 us  [fused_device(): pl.pallas_call(fused_kernel, out_shape=jax.ShapeDtypeStruct((256, HD), bf...]
where the time goes in v4:
time: 45.5 us; the launch traced here: 44.7 us
  Pallas kernels  43.2 us (95%)
  local copies, waits for them, and re-layouts  1.52 us (3%)
    pallas_call x1, Pallas kernels, fused_device(): pl.pallas_call(fused_kernel, out_shape=jax.ShapeDtypeStruct((256, HD), bf...  43.2 us
    unnamed x1, local copies, waits for them, and re-layouts  1.52 us

profile of v4, /device:TPU:0, one launch (start us, length us, event | category | flops | bytes accessed | tf_op | source)
XLA Modules:
  0.0 44.7 jit_solution(2976208801395419004)
XLA Ops:
  0.0 43.2 %shard_map.91 = bf16[256,128]{1,0:T(8,128)(2,1)} custom-call(s32[4]{0:T(128)} %slen_ref.1, s32[8]{0:T(128)} %plen_ref.1, s32[8]{0:T(128)} %pslot_ref.1, s32[64]{0:T(128)} %bitcast.31, bf16[4,64,128]{2,1,0:T(8,128)(2,1)} %bitcast.29, bf16[4,16,128]{2,1,0:T(8,128)(2,1)} %bitcast.30, bf16[4,4096,128]{2,1,0:T(8,128)(2,1)} %bitcast.27, ...), custom_call_target="tpu_custom_call" | custom-call | flops 4000000000 | bytes 12000000 | tf_op jit(solution)/shard_map/pallas_call | solution.py:660
  43.2 1.5 %copy.16 = bf16[32,2,512]{2,1,0:T(2,128)(2,1)} copy(bf16[32,2,512]{2,1,0:T(2,128)(2,1)} %bitcast.26) | data formatting | bytes 131072

commit v5 on v4

--- a/solution.py
+++ b/solution.py
@@ -416,7 +416,7 @@
             half_l[:, :, e] = jnp.broadcast_to(total, (256, HD)).reshape(shape)
 
     def stat_rows(top, total):
-        return jnp.concatenate([top, total], axis=0).T[:8]
+        return jnp.concatenate([top, total], axis=0).T[:1]
 
     def flat(ref, c):
         return ref[c].reshape(PAIR, HD)
@@ -456,6 +456,9 @@
             mine.append(copy)
         swaps.extend(mine)
         prefix_half(h, core)
+        if h == 0:
+            for d in (1, 7, 2, 6, 3, 5, 4):
+                forward(1, d)
         for copy in mine:
             copy.wait_recv()
         for d in (4, 3, 5, 2, 6, 1, 7):
@@ -478,8 +481,6 @@
         co_recv[h][chip], cs_recv[h][chip] = merge(h, chip)
 
     prefix_part(0)
-    for d in (1, 7, 2, 6, 3, 5, 4):
-        forward(1, d)
     prefix_part(1)
     local_part(2)
     local_part(3)
@@ -559,12 +560,12 @@
         pass_z(1, d)
     local_copies[1 + HELD].wait()
     gather_rows(0)
+    for d in (0, 1, 3, 2):
+        pass_x(1, d)
     for n in range(2):
         terms[n] = jnp.dot(
             lhs[:, :2048], w[:2048, n * 256 : (n + 1) * 256], preferred_element_type=f32
         )
-    for d in (0, 1, 3, 2):
-        pass_x(1, d)
     gather_rows(1)
 
     theirs = pl.multiple_of((1 - y) * 64, 64)
@@ -620,7 +621,7 @@
     vm, sm, hbm = pltpu.VMEM, pltpu.SMEM, pl.ANY
     dma = pltpu.SemaphoreType.DMA
     half = (CHIPS, MOST, 2, ROWS, HD)
-    block, stat = vm((2, CHIPS, PAIR, HD), bf16), vm((2, CHIPS, 8, HD), f32)
+    block, stat = vm((2, CHIPS, PAIR, HD), bf16), vm((2, CHIPS, 1, HD), f32)
     scratch = [
         vm((HELD, LOCAL, HD), bf16),
         vm((PSH * 8, HD), bf16),
@@ -645,9 +646,9 @@
         block,
         stat,
         vm((CHIPS, PAIR, HD), bf16),
-        vm((CHIPS, 8, HD), f32),
+        vm((CHIPS, 1, HD), f32),
         vm((CHIPS, PAIR, HD), bf16),
-        vm((CHIPS, 8, HD), f32),
+        vm((CHIPS, 1, HD), f32),
         vm((2, 16, 128, HD), bf16),
         vm((128, 4096), bf16),
         vm((2, 128, 256), f32),

time: 45.5 us -> 44.8 us (0.985)
  no operation moved by 1% of the time
where the time goes in v5:
time: 44.8 us; the launch traced here: 44.5 us
  Pallas kernels  42.9 us (96%)
  local copies, waits for them, and re-layouts  1.52 us (3%)
    pallas_call x1, Pallas kernels, fused_device(): pl.pallas_call(fused_kernel, out_shape=jax.ShapeDtypeStruct((256, HD), bf...  42.9 us
    unnamed x1, local copies, waits for them, and re-layouts  1.52 us

profile of v5, /device:TPU:0, one launch (start us, length us, event | category | flops | bytes accessed | tf_op | source)
XLA Modules:
  0.0 44.5 jit_solution(14021962926994107795)
XLA Ops:
  0.0 42.9 %shard_map.91 = bf16[256,128]{1,0:T(8,128)(2,1)} custom-call(s32[4]{0:T(128)} %slen_ref.1, s32[8]{0:T(128)} %plen_ref.1, s32[8]{0:T(128)} %pslot_ref.1, s32[64]{0:T(128)} %bitcast.31, bf16[4,64,128]{2,1,0:T(8,128)(2,1)} %bitcast.29, bf16[4,16,128]{2,1,0:T(8,128)(2,1)} %bitcast.30, bf16[4,4096,128]{2,1,0:T(8,128)(2,1)} %bitcast.27, ...), custom_call_target="tpu_custom_call" | custom-call | flops 4000000000 | bytes 12000000 | tf_op jit(solution)/shard_map/pallas_call | solution.py:661
  42.9 1.5 %copy.16 = bf16[32,2,512]{2,1,0:T(2,128)(2,1)} copy(bf16[32,2,512]{2,1,0:T(2,128)(2,1)} %bitcast.26) | data formatting | bytes 131072

commit v6 on v5

--- a/solution.py
+++ b/solution.py
@@ -187,8 +187,7 @@
 PART = SPAN // 2
 PAIR = MOST * PART
 SUF_ROWS = SUF * 2 * KVL
-LOCAL = SUF_ROWS + 256
-WING = LOCAL // 2
+LOCAL = SUF_ROWS + 128
 FAR = 1 << 20
 SCALE2 = HD ** (-0.5) * math.log2(math.e)
 NT = (((1,), (1,)), ((), ()))
@@ -360,37 +359,29 @@
             pkv[k, i * 64 : i * 64 + 32, :] = parted[k * 32 : (k + 1) * 32, :HD]
             pkv[k, i * 64 + 32 : (i + 1) * 64, :] = parted[k * 32 : (k + 1) * 32, HD:]
 
-    col = lax.broadcasted_iota(jnp.int32, (2 * SPAN, WING), 1)
-    row = lax.broadcasted_iota(jnp.int32, (2 * SPAN, WING), 0)
-    spot = (col + jnp.where(row < SPAN, 0, WING)) >> 3
+    col = lax.broadcasted_iota(jnp.int32, (SPAN, LOCAL), 1)
+    row = lax.broadcasted_iota(jnp.int32, (SPAN, LOCAL), 0)
+    spot = col >> 3
     fresh = jnp.where(spot - SUF <= (row & 1), -1, FAR)
-    head = (row >> 4) & (KVL - 1)
-    place[...] = jnp.where((col & 7) == head, jnp.where(spot < SUF, spot, fresh), FAR)
-    blank = jnp.zeros((SPAN, HD), bf16)
-
-    def local_part(s):
-        local_copies[1 + s].wait()
-        suf[s, SUF_ROWS : SUF_ROWS + 16, :] = new_ref[s]
-        suf[s, SUF_ROWS + 16 :, :] = jnp.zeros((LOCAL - SUF_ROWS - 16, HD), bf16)
-        wings = jnp.concatenate([suf[s, :WING, :], suf[s, WING:, :]], axis=1)
-        query = jnp.concatenate(
-            [
-                jnp.concatenate([q_ref[s], blank], axis=1),
-                jnp.concatenate([blank, q_ref[s]], axis=1),
-            ],
-            axis=0,
-        )
-        scores = lax.dot_general(query, wings, NT, preferred_element_type=f32)
-        masked = jnp.where(place[...] < slen_ref[s], scores * SCALE2, -1e30)
-        top = jnp.max(masked, axis=1, keepdims=True)
-        top = jnp.maximum(top[:SPAN], top[SPAN:])
-        weights = jnp.exp2(masked - jnp.concatenate([top, top], axis=0))
-        total = jnp.sum(weights, axis=1, keepdims=True)
-        moved = pltpu.roll(weights, KVL, 1).astype(bf16)
-        mixed = jnp.dot(moved, wings, preferred_element_type=f32)
-        lo[s] = mixed[:SPAN, :HD] + mixed[SPAN:, HD:]
-        lm[s] = jnp.broadcast_to(top, (SPAN, HD))
-        ll[s] = jnp.broadcast_to(total[:SPAN] + total[SPAN:], (SPAN, HD))
+    place[...] = jnp.where((col & 7) == (row >> 4), jnp.where(spot < SUF, spot, fresh), FAR)
+
+    def local_part(*samples):
+        for s in samples:
+            local_copies[1 + s].wait()
+            suf[s, SUF_ROWS : SUF_ROWS + 16, :] = new_ref[s]
+            suf[s, SUF_ROWS + 16 :, :] = jnp.zeros((LOCAL - SUF_ROWS - 16, HD), bf16)
+        scores = [
+            lax.dot_general(q_ref[s], suf[s], NT, preferred_element_type=f32) for s in samples
+        ]
+        for s, score in zip(samples, scores):
+            masked = jnp.where(place[...] < slen_ref[s], score * SCALE2, -1e30)
+            top = jnp.max(masked, axis=1, keepdims=True)
+            weights = jnp.exp2(masked - top)
+            total = jnp.sum(weights, axis=1, keepdims=True)
+            moved = pltpu.roll(weights, KVL, 1).astype(bf16)
+            lo[s] = jnp.dot(moved, suf[s], preferred_element_type=f32)
+            lm[s] = jnp.broadcast_to(top, (SPAN, HD))
+            ll[s] = jnp.broadcast_to(total, (SPAN, HD))
 
     local_part(0)
     for d in (1, 7, 2, 6, 3, 5, 4):
@@ -482,8 +473,7 @@
 
     prefix_part(0)
     prefix_part(1)
-    local_part(2)
-    local_part(3)
+    local_part(2, 3)
 
     def attention(h):
         for copy in results[h]:
@@ -629,7 +619,7 @@
         vm((256, 256), bf16),
         vm((128, 128), bf16),
         vm((256, 256), bf16),
-        vm((2 * SPAN, WING), jnp.int32),
+        vm((SPAN, LOCAL), jnp.int32),
         vm((8, PSH, HD), bf16),
         block,
         vm((2, 2, CHIPS, PAIR, HD), bf16),

time: 44.8 us -> 43.5 us (0.971)
  Pallas kernels: 42.9 us -> 41.6 us
    pallas_call x1, Pallas kernels: 42.9 us -> 41.6 us  [fused_device(): pl.pallas_call(fused_kernel, out_shape=jax.ShapeDtypeStruct((256, HD), bf...]
where the time goes in v6:
time: 43.5 us; the launch traced here: 43.1 us
  Pallas kernels  41.6 us (96%)
  local copies, waits for them, and re-layouts  1.52 us (3%)
    pallas_call x1, Pallas kernels, fused_device(): pl.pallas_call(fused_kernel, out_shape=jax.ShapeDtypeStruct((256, HD), bf...  41.6 us
    unnamed x1, local copies, waits for them, and re-layouts  1.52 us

profile of v6, /device:TPU:0, one launch (start us, length us, event | category | flops | bytes accessed | tf_op | source)
XLA Modules:
  0.0 43.1 jit_solution(2598444896681684411)
XLA Ops:
  0.0 41.6 %shard_map.91 = bf16[256,128]{1,0:T(8,128)(2,1)} custom-call(s32[4]{0:T(128)} %slen_ref.1, s32[8]{0:T(128)} %plen_ref.1, s32[8]{0:T(128)} %pslot_ref.1, s32[64]{0:T(128)} %bitcast.31, bf16[4,64,128]{2,1,0:T(8,128)(2,1)} %bitcast.29, bf16[4,16,128]{2,1,0:T(8,128)(2,1)} %bitcast.30, bf16[4,4096,128]{2,1,0:T(8,128)(2,1)} %bitcast.27, ...), custom_call_target="tpu_custom_call" | custom-call | flops 4000000000 | bytes 12000000 | tf_op jit(solution)/shard_map/pallas_call | solution.py:651
  41.6 1.5 %copy.16 = bf16[32,2,512]{2,1,0:T(2,128)(2,1)} copy(bf16[32,2,512]{2,1,0:T(2,128)(2,1)} %bitcast.26) | data formatting | bytes 131072
